TPU v7x, 256 devices: a whole 4x4x8 slice. The times are simulated.
256 devices in a mesh: dp: 4 (over y_hi, core), seq: 64 (over y_lo, z, x).
Axes of the slice: x: 4, y: 4 (y_hi: 2, y_lo: 2; y = y_hi * 2 + y_lo), z: 8, core: 2. Of those that a mesh axis runs over, the one named last changes fastest.
Arguments:
- block_input: bfloat16 [4, 64, 128, 1152], P('dp', 'seq'), may hold values from -6 to 6
- spatial_queries: bfloat16 [4, 64, 128, 576], P('dp', 'seq'), may hold values from -13.5 to 13.5
- spatial_keys: bfloat16 [4, 64, 128, 576], P('dp', 'seq'), may hold values from -4 to 4
- cotangent: bfloat16 [4, 64, 128, 1152], P('dp', None, 'seq'), may hold values from -16 to 16
- temporal_queries: bfloat16 [4, 64, 128, 576], P('dp', None, 'seq'), may hold values from -13.5 to 13.5
- temporal_keys: bfloat16 [4, 64, 128, 576], P('dp', None, 'seq'), may hold values from -4 to 4
- weights: bfloat16 [4, 1152, 576], replicated, may hold values from -0.1875 to 0.1875
Outputs:
- input_grad: bfloat16 [4, 64, 128, 1152], P('dp', 'seq')
- spatial_query_grad: bfloat16 [4, 64, 128, 576], P('dp', 'seq')
- spatial_key_grad: bfloat16 [4, 64, 128, 576], P('dp', 'seq')
- temporal_query_grad: bfloat16 [4, 64, 128, 576], P('dp', None, 'seq')
- temporal_key_grad: bfloat16 [4, 64, 128, 576], P('dp', None, 'seq')
- weight_grads: float32 [4, 1152, 576], P(None, 'seq', 'dp')
All inputs are finite; a program needn't handle non-finite values.
Results may differ from a plain program's by a relative error of at most 0.014.
Values may be sent and summed in bfloat16 or wider, within the bound.
A program may use at most 128 MiB of HBM per device.

v0:
```python
import jax
import jax.numpy as jnp
from jax import lax
from jax.sharding import PartitionSpec as P

HEADS = 8
HEAD_DIM = 72


def project(einsum_form, left_side, right_side):
    return jnp.einsum(einsum_form, left_side, right_side, preferred_element_type=jnp.float32)


def with_heads(tensor):
    return tensor.reshape(tensor.shape[:-1] + (HEADS, HEAD_DIM))


def without_heads(tensor):
    return tensor.reshape(tensor.shape[:-2] + (HEADS * HEAD_DIM,))


def chances(queries, key_rows):
    scores = project("xlyhe,xmyhe->xyhlm", queries, key_rows) * HEAD_DIM ** (-0.5)
    return jax.nn.softmax(scores, axis=-1)


def attend(prob_map, values):
    return project("xyhlm,xmyhe->xlyhe", prob_map.astype(jnp.bfloat16), values).astype(jnp.bfloat16)


def attend_back(prob_map, queries, key_rows, values, out_grad):
    rounded = prob_map.astype(jnp.bfloat16)
    prob_grad = project("xlyhe,xmyhe->xyhlm", out_grad, values)
    value_grad = project("xyhlm,xlyhe->xmyhe", rounded, out_grad).astype(jnp.bfloat16)
    centre = jnp.sum(prob_map * prob_grad, axis=-1, keepdims=True)
    score_grad = (prob_map * (prob_grad - centre)).astype(jnp.bfloat16)
    query_grad = (project("xyhlm,xmyhe->xlyhe", score_grad, key_rows) * HEAD_DIM ** (-0.5)).astype(
        jnp.bfloat16
    )
    key_grad = (project("xyhlm,xlyhe->xmyhe", score_grad, queries) * HEAD_DIM ** (-0.5)).astype(
        jnp.bfloat16
    )
    return (query_grad, key_grad, value_grad)


def reduce_grads(terms):
    row_share = lax.psum_scatter(terms, "seq", scatter_dimension=1, tiled=True)
    return lax.psum_scatter(
        row_share.astype(jnp.bfloat16), "dp", scatter_dimension=2, tiled=True
    ).astype(jnp.float32)


def body(
    block_input, spatial_queries, spatial_keys, cotangent, temporal_queries, temporal_keys, weights
):
    clip_count, frame_count, patch_count, model_width = block_input.shape
    grad_scale = float(
        clip_count * lax.axis_size("dp") * frame_count * lax.axis_size("seq") * patch_count
    ) ** (-0.5)

    def spatial_view(tensor):
        return tensor.reshape(clip_count * frame_count, patch_count, 1, HEADS, HEAD_DIM)

    def spatial_flat(tensor):
        return tensor.reshape(clip_count, frame_count, patch_count, HEADS * HEAD_DIM)

    query_sp = spatial_view(spatial_queries)
    key_sp = spatial_view(spatial_keys)
    value_sp = project("cfpd,de->cfpe", block_input, weights[0]).astype(jnp.bfloat16)
    prob_sp = chances(query_sp, key_sp)
    attended = spatial_flat(attend(prob_sp, spatial_view(value_sp)))
    mixed = (
        block_input.astype(jnp.float32) + project("cfpe,de->cfpd", attended, weights[1])
    ).astype(jnp.bfloat16)
    mixed_tm = lax.all_to_all(mixed, "seq", split_axis=2, concat_axis=1, tiled=True)
    value_tm = project("cfpd,de->cfpe", mixed_tm, weights[2]).astype(jnp.bfloat16)
    query_heads = with_heads(temporal_queries)
    key_heads = with_heads(temporal_keys)
    prob_tm = chances(query_heads, key_heads)
    attended_tm = without_heads(attend(prob_tm, with_heads(value_tm)))
    out_weight_tm = project("cfpd,cfpe->de", cotangent, attended_tm)
    attended_tm_grad = project("cfpd,de->cfpe", cotangent, weights[3]).astype(jnp.bfloat16)
    query_tm_grad, key_tm_grad, value_tm_grad = attend_back(
        prob_tm, query_heads, key_heads, with_heads(value_tm), with_heads(attended_tm_grad)
    )
    value_tm_grad = without_heads(value_tm_grad)
    value_weight_tm = project("cfpd,cfpe->de", mixed_tm, value_tm_grad)
    mixed_tm_grad = (
        cotangent.astype(jnp.float32) + project("cfpe,de->cfpd", value_tm_grad, weights[2])
    ).astype(jnp.bfloat16)
    mixed_grad = lax.all_to_all(mixed_tm_grad, "seq", split_axis=1, concat_axis=2, tiled=True)
    temporal_share = reduce_grads(jnp.stack([value_weight_tm, out_weight_tm]) * grad_scale)
    out_weight_sp = project("cfpd,cfpe->de", mixed_grad, attended)
    attended_grad = project("cfpd,de->cfpe", mixed_grad, weights[1]).astype(jnp.bfloat16)
    query_sp_grad, key_sp_grad, value_sp_grad = attend_back(
        prob_sp, query_sp, key_sp, spatial_view(value_sp), spatial_view(attended_grad)
    )
    value_sp_grad = spatial_flat(value_sp_grad)
    value_weight_sp = project("cfpd,cfpe->de", block_input, value_sp_grad)
    input_grad = (
        mixed_grad.astype(jnp.float32) + project("cfpe,de->cfpd", value_sp_grad, weights[0])
    ).astype(jnp.bfloat16)
    spatial_share = reduce_grads(jnp.stack([value_weight_sp, out_weight_sp]) * grad_scale)
    weight_grads = jnp.concatenate([spatial_share, temporal_share], axis=0)
    return (
        input_grad,
        spatial_flat(query_sp_grad),
        spatial_flat(key_sp_grad),
        without_heads(query_tm_grad),
        without_heads(key_tm_grad),
        weight_grads,
    )


def solution(mesh):
    placed = (
        P("dp", "seq", None, None),
        P("dp", "seq", None, None),
        P("dp", "seq", None, None),
        P("dp", None, "seq", None),
        P("dp", None, "seq", None),
        P("dp", None, "seq", None),
        P(),
    )
    return jax.shard_map(
        body,
        mesh=mesh,
        in_specs=placed,
        out_specs=(
            P("dp", "seq", None, None),
            P("dp", "seq", None, None),
            P("dp", "seq", None, None),
            P("dp", None, "seq", None),
            P("dp", None, "seq", None),
            P(None, "seq", "dp"),
        ),
        check_vma=False,
    )
```

profile of v0, /device:TPU:4, one launch (start us, length us, event | category | flops | bytes accessed | tf_op | source)
XLA Modules:
  0.0 568.2 jit_solution(11692212553838512160)
XLA Ops:
  7.2 2.0 fusion.36
  9.5 1.2 reshape.250
  10.8 1.3 reshape.249
  12.5 0.8 copy-done.8
  13.9 1.7 fusion.4
  15.6 1.0 copy.122
  16.6 13.0 %all-to-all-start = ((bf16[1,64,2,1152]{3,2,0,1:T(2,128)(2,1)}), bf16[1,64,2,1152]{3,2,0,1:T(2,128)(2,1)S(1)}, u32[]{:S(2)}, u32[]{:S(2)}) async-start(bf16[1,64,2,1152]{3,2,0,1:T(2,128)(2,1)} %copy.122), calls=%async_computation | async-start | bytes 589824 | tf_op jit(solution)/shard_map/all_to_all | solution.py:91
  29.6 1.8 fusion.47
  31.9 0.5 convolution_convert_fusion.2
  32.4 1.8 fusion.5
  34.7 0.5 broadcast.61
  35.2 2.4 reduce.14
  37.6 0.8 reshape.279
  38.5 0.6 dynamic-slice
  39.7 2.3 all-to-all-done
  42.0 9.0 %all-to-all-start.1 = ((bf16[64,2,1152]{2,1,0:T(2,128)(2,1)}), bf16[64,2,1152]{2,1,0:T(2,128)(2,1)S(1)}, u32[]{:S(2)}, u32[]{:S(2)}) async-start(bf16[64,2,1152]{2,1,0:T(2,128)(2,1)} %reshape.279), calls=%async_computation.1 | async-start | bytes 589824 | tf_op jit(solution)/shard_map/all_to_all | solution.py:75
  51.4 1.8 fusion.44
  53.2 1.2 multiply_reduce_fusion.1
  54.5 1.2 convolution_convert_fusion.3
  55.8 0.9 fusion.42
  56.7 1.0 fusion.43
  57.6 5.2 all-to-all-done.1
  63.0 1.7 bitcast_reduce_fusion
  64.8 1.9 fusion.39
  67.0 1.1 multiply_reduce_fusion
  68.4 2.0 convolution_bitcast_fusion.2
  71.0 2.5 fusion.7
  73.4 2.0 convolution_bitcast_fusion.3
  75.9 1.6 convolution_bitcast_fusion.1
  77.7 2.8 maximum_multiply_fusion.1
  80.5 11.4 %copy.142 = f32[2,1152,576]{2,0,1:T(2,128)} copy(f32[2,1152,576]{1,2,0:T(8,128)} %maximum_multiply_fusion.1) | data formatting | bytes 10616832 | tf_op jit(solution)/shard_map/mul | solution.py:92
  91.9 4.5 maximum_multiply_fusion
  96.4 11.4 %copy.136 = f32[2,1152,576]{2,0,1:T(2,128)} copy(f32[2,1152,576]{1,2,0:T(8,128)} %maximum_multiply_fusion) | data formatting | bytes 10616832 | tf_op jit(solution)/shard_map/mul | solution.py:103
  107.8 373.3 %all-reduce.4 = (bf16[2,1152,576]{2,0,1:T(2,128)(2,1)}, bf16[2,1152,576]{2,0,1:T(2,128)(2,1)}) all-reduce(f32[2,1152,576]{2,0,1:T(2,128)} %copy.142, f32[2,1152,576]{2,0,1:T(2,128)} %copy.136), channel_id=4, replica_groups=mesh['dp'=4,'seq'=64] {'seq'}, use_global_device_ids=true, to_apply=%region_8.0.clone | all-reduce | flops 2654208 | bytes 15925248
  481.1 0.9 dynamic-slice_convert_fusion
  482.0 3.7 copy.155
  485.7 4.6 reshape.274
  491.2 1.2 reshape.270
  492.3 3.6 copy.153
  496.0 4.6 reshape.272
  501.0 1.2 reshape.271
  502.1 22.8 %reduce-scatter.9.cloned.1.call-done = bf16[144,36]{1,0:T(8,128)(2,1)} async-done(((bf16[576,36]{1,0:T(8,128)(2,1)}), bf16[144,36]{1,0:T(8,128)(2,1)}) %reduce-scatter.9.cloned.1.call-update) | async-done | bytes 10384
  525.0 1.3 reshape.275
  526.2 0.6 copy.156
  526.8 32.0 %reduce-scatter.7.cloned.1.call-done = bf16[144,36]{1,0:T(8,128)(2,1)} async-done(((bf16[576,36]{1,0:T(8,128)(2,1)}), bf16[144,36]{1,0:T(8,128)(2,1)}) %reduce-scatter.7.cloned.1.call-update) | async-done | bytes 10384
  558.8 1.3 reshape.273
  560.1 0.6 copy.154
  560.7 0.7 maximum_convert_fusion
  (58 shorter events, 5.7 us)
Async XLA Ops:
  7.2 24.3 %copy-start = (bf16[1,1,128,576]{2,3,1,0:T(8,128)(2,1)S(1)}, bf16[1,1,128,576]{2,3,1,0:T(8,128)(2,1)}, u32[]{:S(2)}) copy-start(bf16[1,1,128,576]{2,3,1,0:T(8,128)(2,1)} %param.9) | copy-start | bytes 442372
  7.2 6.7 %copy-start.12 = (bf16[1,64,2,1152]{3,2,1,0:T(2,128)(2,1)S(1)}, bf16[1,64,2,1152]{3,2,1,0:T(2,128)(2,1)}, u32[]{:S(2)}) copy-start(bf16[1,64,2,1152]{3,2,1,0:T(2,128)(2,1)} %param.10) | copy-start | bytes 884740
  10.8 4.8 copy-start.5
  12.1 4.5 copy-start.3
  12.4 0.8 copy-start.8
  12.4 17.2 %copy-start.2 = (bf16[1,1,128,1152]{3,2,1,0:T(8,128)(2,1)S(1)}, bf16[1,1,128,1152]{3,2,1,0:T(8,128)(2,1)}, u32[]{:S(2)}) copy-start(bf16[1,1,128,1152]{3,2,1,0:T(8,128)(2,1)} %param.7) | copy-start | bytes 884740
  13.5 18.0 %copy-start.13 = (bf16[1,1,128,576]{2,3,1,0:T(8,128)(2,1)S(1)}, bf16[1,1,128,576]{2,3,1,0:T(8,128)(2,1)}, u32[]{:S(2)}) copy-start(bf16[1,1,128,576]{2,3,1,0:T(8,128)(2,1)} %param.8) | copy-start | bytes 442372
  16.6 25.4 %all-to-all-start = ((bf16[1,64,2,1152]{3,2,0,1:T(2,128)(2,1)}), bf16[1,64,2,1152]{3,2,0,1:T(2,128)(2,1)S(1)}, u32[]{:S(2)}, u32[]{:S(2)}) async-start(bf16[1,64,2,1152]{3,2,0,1:T(2,128)(2,1)} %copy.122), calls=%async_computation | async-start | bytes 589824 | tf_op jit(solution)/shard_map/all_to_all | solution.py:91
  31.5 6.1 %copy-start.15 = (bf16[128,576]{0,1:T(8,128)(2,1)}, bf16[128,576]{0,1:T(8,128)(2,1)S(1)}, u32[]{:S(2)}) copy-start(bf16[128,576]{0,1:T(8,128)(2,1)S(1)} %fusion.47) | copy-start | bytes 442372
  31.9 6.6 %copy-start.16 = (u32[256]{0:T(256)S(1)}, u32[256]{0:T(256)}, u32[]{:S(2)}) copy-start(u32[256]{0:T(256)} %constant.21) | copy-start | bytes 3076
  37.6 16.9 %copy-start.14 = (bf16[1,1,128,576]{2,3,1,0:T(8,128)(2,1)S(1)}, bf16[1,1,128,576]{2,3,1,0:T(8,128)(2,1)}, u32[]{:S(2)}) copy-start(bf16[1,1,128,576]{2,3,1,0:T(8,128)(2,1)} %param.8) | copy-start | bytes 442372
  42.0 20.8 %all-to-all-start.1 = ((bf16[64,2,1152]{2,1,0:T(2,128)(2,1)}), bf16[64,2,1152]{2,1,0:T(2,128)(2,1)S(1)}, u32[]{:S(2)}, u32[]{:S(2)}) async-start(bf16[64,2,1152]{2,1,0:T(2,128)(2,1)} %reshape.279), calls=%async_computation.1 | async-start | bytes 589824 | tf_op jit(solution)/shard_map/all_to_all | solution.py:75
  51.0 473.9 %reduce-scatter.9.cloned.1.call-start = ((), (), s32[]{:S(2)}) async-start(), calls=%async_computation.5 | async-start | bytes 184320
  55.8 11.3 %copy-start.9 = (f32[2,8,64,64]{2,3,1,0:T(8,128)S(1)}, f32[2,8,64,64]{2,3,1,0:T(8,128)}, u32[]{:S(2)}) copy-start(f32[2,8,64,64]{2,3,1,0:T(8,128)} %copy-done.8) | copy-start | bytes 786436
  68.4 2.5 copy-start.7
  75.9 1.8 copy-start.1
  482.0 8.6 %copy-start.10 = (f32[2,8,64,64]{2,3,1,0:T(8,128)S(1)}, f32[2,8,64,64]{2,3,1,0:T(8,128)}, u32[]{:S(2)}) copy-start(f32[2,8,64,64]{2,3,1,0:T(8,128)} %copy-done.8) | copy-start | bytes 786436
  482.0 8.6 %copy-start.11 = (f32[2,8,64,64]{2,3,1,0:T(8,128)S(1)}, f32[2,8,64,64]{2,3,1,0:T(8,128)}, u32[]{:S(2)}) copy-start(f32[2,8,64,64]{2,3,1,0:T(8,128)} %get-tuple-element.45) | copy-start | bytes 786436
  482.0 8.7 %copy-start.6 = (bf16[64,2,8,72]{3,2,1,0:T(8,128)(2,1)S(1)}, bf16[64,2,8,72]{3,2,1,0:T(8,128)(2,1)}, u32[]{:S(2)}) copy-start(bf16[64,2,8,72]{3,2,1,0:T(8,128)(2,1)} %copy-done.5) | copy-start | bytes 442372
  490.3 68.5 %reduce-scatter.7.cloned.1.call-start = ((), (), s32[]{:S(2)}) async-start(), calls=%async_computation.4 | async-start | bytes 184320
  492.3 8.2 %copy-start.4 = (bf16[64,2,8,72]{3,2,1,0:T(8,128)(2,1)S(1)}, bf16[64,2,8,72]{3,2,1,0:T(8,128)(2,1)}, u32[]{:S(2)}) copy-start(bf16[64,2,8,72]{3,2,1,0:T(8,128)(2,1)} %copy-done.3) | copy-start | bytes 442372
Sparse Core Ops, SparseCore 0:
  490.4 34.5 reduce-scatter.8
  527.7 31.1 reduce-scatter.6
where the time goes:
time: 570 us; the launch traced here: 568 us
  blocking collectives  373 us (65%)
  waiting for transfers between devices  62.3 us (11%)
  local copies, waits for them, and re-layouts  56.8 us (10%)
  matrix products  27.4 us (5%)
  starting transfers between devices  22.5 us (4%)
  between operations  15.2 us (3%)
  other arithmetic  10.6 us (2%)
    unnamed x1, blocking collectives  373 us
    unnamed x4, waiting for transfers between devices  54.9 us
    dot_general x21, matrix products, project(): jnp.einsum(einsum_form, left_side, right_side, preferred_element_type=jnp...  26.7 us
    unnamed x50, local copies, waits for them, and re-layouts  26 us
    all_to_all x1, starting transfers between devices, body(): lax.all_to_all(mixed_tm_grad, 'seq', split_axis=1, concat_axis=2, tiled=T...  13 us
    mul x1, local copies, waits for them, and re-layouts, body(): jnp.stack([value_weight_sp, out_weight_sp]) * grad_scale  11.4 us
  transfers between devices with their start and end apart: 4, of which 4 were waited for; matrix products, arithmetic and copies ran while one was open for 5% of the time, Pallas kernels for 0%

commit v1 on v0

--- a/solution.py
+++ b/solution.py
@@ -44,10 +44,17 @@
 
 
 def reduce_grads(terms):
-    row_share = lax.psum_scatter(terms, "seq", scatter_dimension=1, tiled=True)
-    return lax.psum_scatter(
-        row_share.astype(jnp.bfloat16), "dp", scatter_dimension=2, tiled=True
-    ).astype(jnp.float32)
+    count, rows, columns = terms.shape
+    over_dp, over_seq = lax.axis_size("dp"), lax.axis_size("seq")
+    blocks = terms.astype(jnp.bfloat16).reshape(
+        count, over_seq, rows // over_seq, over_dp, columns // over_dp
+    )
+    blocks = blocks.transpose(3, 1, 0, 2, 4).reshape(over_dp, over_seq, -1)
+    blocks = lax.all_to_all(blocks, "dp", split_axis=0, concat_axis=0, tiled=True)
+    part = jnp.sum(blocks.astype(jnp.float32), axis=0).astype(jnp.bfloat16)
+    part = lax.all_to_all(part, "seq", split_axis=0, concat_axis=0, tiled=True)
+    share = jnp.sum(part.astype(jnp.float32), axis=0)
+    return share.reshape(count, rows // over_seq, columns // over_dp)
 
 
 def body(
@@ -89,7 +96,6 @@
         cotangent.astype(jnp.float32) + project("cfpe,de->cfpd", value_tm_grad, weights[2])
     ).astype(jnp.bfloat16)
     mixed_grad = lax.all_to_all(mixed_tm_grad, "seq", split_axis=1, concat_axis=2, tiled=True)
-    temporal_share = reduce_grads(jnp.stack([value_weight_tm, out_weight_tm]) * grad_scale)
     out_weight_sp = project("cfpd,cfpe->de", mixed_grad, attended)
     attended_grad = project("cfpd,de->cfpe", mixed_grad, weights[1]).astype(jnp.bfloat16)
     query_sp_grad, key_sp_grad, value_sp_grad = attend_back(
@@ -100,8 +106,9 @@
     input_grad = (
         mixed_grad.astype(jnp.float32) + project("cfpe,de->cfpd", value_sp_grad, weights[0])
     ).astype(jnp.bfloat16)
-    spatial_share = reduce_grads(jnp.stack([value_weight_sp, out_weight_sp]) * grad_scale)
-    weight_grads = jnp.concatenate([spatial_share, temporal_share], axis=0)
+    weight_grads = reduce_grads(
+        jnp.stack([value_weight_sp, out_weight_sp, value_weight_tm, out_weight_tm]) * grad_scale
+    )
     return (
         input_grad,
         spatial_flat(query_sp_grad),

time: 570 us -> 254 us (0.45)
  blocking collectives: 373 us -> 67.7 us
  waiting for transfers between devices: 62.3 us -> 34.2 us
  local copies, waits for them, and re-layouts: 56.8 us -> 78.3 us
  between operations: 15.2 us -> 1.22 us
    unnamed x1 -> x0, blocking collectives: 373 us -> none
    all_to_all x0 -> x1, blocking collectives: none -> 67.7 us  [reduce_grads(): lax.all_to_all(blocks, 'dp', split_axis=0, concat_axis=0, tiled=True)]
    unnamed x4 -> x0, waiting for transfers between devices: 54.9 us -> none
    all_to_all x0 -> x1, waiting for transfers between devices: none -> 23.8 us  [reduce_grads(): part = lax.all_to_all(part, 'seq', split_axis=0, concat_axis=0, tiled=True)]
    mul x2 -> x0, local copies, waits for them, and re-layouts: 22.8 us -> none  [the longest x1 11.4 us: body(): jnp.stack([value_weight_sp, out_weight_sp]) * grad_scale]
    another operation x7 -> x12, local copies, waits for them, and re-layouts: 3.58 us -> 21.8 us  [the longest x4 19.4 us: body(): jnp.stack([value_weight_sp, out_weight_sp, value_weight_tm, out_weight_tm])]
    reshape x0 -> x2, local copies, waits for them, and re-layouts: none -> 18.1 us  [the longest x1 18 us: reduce_grads(): blocks = blocks.transpose(3, 1, 0, 2, 4).reshape(over_dp, over_seq, -1)]
    transpose x0 -> x1, local copies, waits for them, and re-layouts: none -> 9.09 us  [reduce_grads(): blocks = blocks.transpose(3, 1, 0, 2, 4).reshape(over_dp, over_seq, -1)]
  transfers between devices with their start and end apart: 4 -> 3, of which waited for: 4 -> 3; matrix products, arithmetic and copies ran while one was open for 5% -> 9% of each run, Pallas kernels for 0% -> 0%
where the time goes in v1:
time: 254 us; the launch traced here: 251 us
  local copies, waits for them, and re-layouts  78.3 us (31%)
  blocking collectives  67.7 us (27%)
  waiting for transfers between devices  34.2 us (13%)
  matrix products  28.9 us (11%)
  starting transfers between devices  27 us (11%)
  other arithmetic  13.4 us (5%)
    all_to_all x1, blocking collectives, reduce_grads(): lax.all_to_all(blocks, 'dp', split_axis=0, concat_axis=0, tiled=True)  67.7 us
    dot_general x21, matrix products, project(): jnp.einsum(einsum_form, left_side, right_side, preferred_element_type=jnp...  26.5 us
    all_to_all x1, waiting for transfers between devices, reduce_grads(): part = lax.all_to_all(part, 'seq', split_axis=0, concat_axis=0, tiled=True)  23.8 us
    another operation x4, local copies, waits for them, and re-layouts, body(): jnp.stack([value_weight_sp, out_weight_sp, value_weight_tm, out_weight_tm])  19.4 us
    reshape x1, local copies, waits for them, and re-layouts, reduce_grads(): blocks = blocks.transpose(3, 1, 0, 2, 4).reshape(over_dp, over_seq, -1)  18 us
    unnamed x68, local copies, waits for them, and re-layouts  17.4 us
    all_to_all x1, starting transfers between devices, body(): lax.all_to_all(mixed, 'seq', split_axis=2, concat_axis=1, tiled=True)  13 us
    transpose x1, local copies, waits for them, and re-layouts, reduce_grads(): blocks = blocks.transpose(3, 1, 0, 2, 4).reshape(over_dp, over_seq, -1)  9.09 us
  transfers between devices with their start and end apart: 3, of which 3 were waited for; matrix products, arithmetic and copies ran while one was open for 9% of the time, Pallas kernels for 0%

profile of v1, /device:TPU:4, one launch (start us, length us, event | category | flops | bytes accessed | tf_op | source)
XLA Modules:
  0.0 250.6 jit_solution(9021190801717485272)
XLA Ops:
  0.7 2.0 fusion.49
  2.7 2.1 fusion.91
  4.8 1.5 convolution_convert_fusion.2
  6.3 1.8 fusion.7
  9.1 2.4 reduce.16
  11.5 0.8 reshape.313
  12.3 13.0 %all-to-all-start.1 = ((bf16[64,2,1152]{2,1,0:T(2,128)(2,1)}), bf16[64,2,1152]{2,1,0:T(2,128)(2,1)S(1)}, u32[]{:S(2)}, u32[]{:S(2)}) async-start(bf16[64,2,1152]{2,1,0:T(2,128)(2,1)} %reshape.313), calls=%async_computation.1 | async-start | bytes 589824 | tf_op jit(solution)/shard_map/all_to_all | solution.py:82
  25.3 1.9 fusion.38
  29.7 0.9 dot_general.122
  30.7 1.7 fusion.6
  32.4 1.0 copy.111
  33.4 4.2 %all-to-all-done.1 = bf16[64,2,1152]{2,1,0:T(2,128)(2,1)S(1)} async-done(((bf16[64,2,1152]{2,1,0:T(2,128)(2,1)}), bf16[64,2,1152]{2,1,0:T(2,128)(2,1)S(1)}, u32[]{:S(2)}, u32[]{:S(2)}) %all-to-all-start.1) | async-done | bytes 294944 | tf_op jit(solution)/shard_map/all_to_all | solution.py:82
  37.6 7.1 %all-to-all-start = ((bf16[1,64,2,1152]{3,2,0,1:T(2,128)(2,1)}), bf16[1,64,2,1152]{3,2,0,1:T(2,128)(2,1)S(1)}, u32[]{:S(2)}, u32[]{:S(2)}) async-start(bf16[1,64,2,1152]{3,2,0,1:T(2,128)(2,1)} %copy.111), calls=%async_computation | async-start | bytes 589824 | tf_op jit(solution)/shard_map/all_to_all | solution.py:98
  45.0 1.7 bitcast_reduce_fusion
  46.8 1.9 fusion.41
  49.0 0.7 copy-done.18
  50.4 6.1 %all-to-all-done = bf16[1,64,2,1152]{3,2,0,1:T(2,128)(2,1)S(1)} async-done(((bf16[1,64,2,1152]{3,2,0,1:T(2,128)(2,1)}), bf16[1,64,2,1152]{3,2,0,1:T(2,128)(2,1)S(1)}, u32[]{:S(2)}, u32[]{:S(2)}) %all-to-all-start) | async-done | bytes 294944 | tf_op jit(solution)/shard_map/all_to_all | solution.py:98
  56.6 1.8 fusion.46
  58.5 1.2 convolution_convert_fusion.3
  59.9 0.8 reshape.297
  60.8 1.8 copy.128
  62.6 2.0 convolution_bitcast_fusion
  64.6 2.7 %copy.135 = f32[1152,576]{1,0:T(8,128)S(1)} copy(f32[1152,576]{0,1:T(8,128)} %convolution_bitcast_fusion) | data formatting | bytes 5308416 | tf_op jit(solution)/shard_map/cfpd,cfpe->de/dot_general | solution.py:11
  67.3 4.7 %stack.12 = f32[1,64,18,4,144]{4,3,2,1,0:T(4,128)} reshape(f32[1152,576]{1,0:T(8,128)S(1)} %copy.135) | data formatting | bytes 5308416 | tf_op jit(solution)/shard_map/stack | solution.py:110
  72.0 6.0 %copy.137 = f32[1,64,18,4,144]{4,1,3,2,0:T(8,128)} copy(f32[1,64,18,4,144]{4,3,2,1,0:T(4,128)} %stack.12) | data formatting | bytes 5308416 | tf_op jit(solution)/shard_map/stack | solution.py:110
  78.1 2.0 convolution_bitcast_fusion.1
  80.1 2.7 %copy.125 = f32[1152,576]{1,0:T(8,128)S(1)} copy(f32[1152,576]{0,1:T(8,128)} %convolution_bitcast_fusion.1) | data formatting | bytes 5308416 | tf_op jit(solution)/shard_map/cfpd,cfpe->de/dot_general | solution.py:11
  82.8 4.7 %stack.11 = f32[1,64,18,4,144]{4,3,2,1,0:T(4,128)} reshape(f32[1152,576]{1,0:T(8,128)S(1)} %copy.125) | data formatting | bytes 5308416 | tf_op jit(solution)/shard_map/stack | solution.py:110
  87.5 3.9 %copy.136 = f32[1,64,18,4,144]{4,1,3,2,0:T(8,128)S(1)} copy(f32[1,64,18,4,144]{4,3,2,1,0:T(4,128)} %stack.11) | data formatting | bytes 5308416 | tf_op jit(solution)/shard_map/stack | solution.py:110
  91.5 0.8 convolution_bitcast_fusion.4
  92.4 0.8 convolution_bitcast_fusion.5
  93.9 2.9 %fusion.3 = bf16[4,64,4,18,144]{4,1,0,3,2:T(8,128)(2,1)S(1)} fusion(f32[1,64,18,4,144]{4,1,3,2,0:T(8,128)S(1)} %bitcast.180, f32[1,64,18,4,144]{4,1,3,2,0:T(8,128)S(1)} %convolution_bitcast_fusion.4, f32[1,64,18,4,144]{4,1,3,2,0:T(8,128)S(1)} %convolution_bitcast_fusion.5, f32[1,64,18,4,144]{4,1,3,2,0:T(8,128)S(1)} %copy.136), kind=kLoop, calls=%fused_computation.4 | loop fusion | flops 13271040 | bytes 15925248 | tf_op jit(solution)/shard_map/transpose | solution.py:52
  96.8 9.1 %copy.138 = bf16[4,64,4,18,144]{4,3,2,1,0:T(8,128)(2,1)} copy(bf16[4,64,4,18,144]{4,1,0,3,2:T(8,128)(2,1)S(1)} %fusion.3) | data formatting | bytes 10616832 | tf_op jit(solution)/shard_map/transpose | solution.py:52
  105.9 18.0 %reshape.300 = bf16[4,64,10368]{2,1,0:T(8,128)(2,1)} reshape(bf16[4,64,4,18,144]{4,3,2,1,0:T(8,128)(2,1)} %copy.138) | data formatting | bytes 10616832 | tf_op jit(solution)/shard_map/reshape | solution.py:52
  123.9 67.7 %all_to_all.35 = bf16[4,64,10368]{2,1,0:T(8,128)(2,1)} all-to-all(bf16[4,64,10368]{2,1,0:T(8,128)(2,1)} %reshape.300), channel_id=1, replica_groups=mesh['dp'=4,'seq'=64] {'dp'}, dimensions={0} | all-to-all | bytes 10616832 | tf_op jit(solution)/shard_map/all_to_all | solution.py:53
  191.6 3.5 %reduce_sum.61 = bf16[64,10368]{1,0:T(8,128)(2,1)S(1)} reduce(bf16[4,64,10368]{2,1,0:T(8,128)(2,1)} %all_to_all.35, bf16[]{:T(256)} %constant.1.clone.1), dimensions={0}, to_apply=%region_6.0 | reduce | flops 1990656 | bytes 6635522 | tf_op jit(solution)/shard_map/reduce_sum | solution.py:54
  195.0 1.7 reduce.17
  196.7 2.1 reshape.315
  198.8 6.9 %all-to-all-start.3 = ((bf16[64,2,5184]{2,1,0:T(2,128)(2,1)}), bf16[64,2,5184]{2,1,0:T(2,128)(2,1)}, u32[]{:S(2)}, u32[]{:S(2)}) async-start(bf16[64,2,5184]{2,1,0:T(2,128)(2,1)} %reshape.315), calls=%async_computation.3 | async-start | bytes 2686976 | tf_op jit(solution)/shard_map/all_to_all | solution.py:55
  205.8 1.4 multiply_reduce_fusion
  207.8 1.2 reshape.310
  209.3 1.2 reshape.311
  210.5 2.5 fusion.9
  213.4 1.0 fusion.45
  214.4 0.9 fusion.44
  215.3 23.8 %all-to-all-done.3 = bf16[64,2,5184]{2,1,0:T(2,128)(2,1)} async-done(((bf16[64,2,5184]{2,1,0:T(2,128)(2,1)}), bf16[64,2,5184]{2,1,0:T(2,128)(2,1)}, u32[]{:S(2)}, u32[]{:S(2)}) %all-to-all-start.3) | async-done | bytes 1327136 | tf_op jit(solution)/shard_map/all_to_all | solution.py:55
  239.1 8.0 %reshape.316 = bf16[64,1,10368]{2,1,0:T(2,128)(2,1)S(1)} reshape(bf16[64,2,5184]{2,1,0:T(2,128)(2,1)} %all-to-all-done.3) | data formatting | bytes 2654208
  247.2 2.7 %convert_reduce_fusion = f32[10368]{0:T(1024)S(1)} fusion(bf16[64,1,10368]{2,1,0:T(2,128)(2,1)S(1)} %reshape.316), kind=kLoop, calls=%fused_computation.7 | loop fusion | flops 1316736 | bytes 1368576 | tf_op jit(solution)/shard_map/reduce_sum | solution.py:56
  (84 shorter events, 8.0 us)
Async XLA Ops:
  0.6 2.0 copy-start
  0.6 5.7 %copy-start.3 = (bf16[1,1,128,1152]{3,2,1,0:T(8,128)(2,1)S(1)}, bf16[1,1,128,1152]{3,2,1,0:T(8,128)(2,1)}, u32[]{:S(2)}) copy-start(bf16[1,1,128,1152]{3,2,1,0:T(8,128)(2,1)} %param.7) | copy-start | bytes 884740
  2.6 3.7 %copy-start.23 = (bf16[128,576]{0,1:T(8,128)(2,1)}, bf16[128,576]{0,1:T(8,128)(2,1)S(1)}, u32[]{:S(2)}) copy-start(bf16[128,576]{0,1:T(8,128)(2,1)S(1)} %fusion.49) | copy-start | bytes 442372
  2.6 22.6 %copy-start.16 = (bf16[1,64,2,1152]{3,2,1,0:T(2,128)(2,1)S(1)}, bf16[1,64,2,1152]{3,2,1,0:T(2,128)(2,1)}, u32[]{:S(2)}) copy-start(bf16[1,64,2,1152]{3,2,1,0:T(2,128)(2,1)} %param.10) | copy-start | bytes 884740
  4.8 22.4 %copy-start.19 = (bf16[1,64,2,576]{3,2,1,0:T(2,128)(2,1)S(1)}, bf16[1,64,2,576]{3,2,1,0:T(2,128)(2,1)}, u32[]{:S(2)}) copy-start(bf16[1,64,2,576]{3,2,1,0:T(2,128)(2,1)} %param.11) | copy-start | bytes 442372
  4.8 22.7 %copy-start.20 = (bf16[1,64,2,576]{3,2,1,0:T(2,128)(2,1)S(1)}, bf16[1,64,2,576]{3,2,1,0:T(2,128)(2,1)}, u32[]{:S(2)}) copy-start(bf16[1,64,2,576]{3,2,1,0:T(2,128)(2,1)} %param.12) | copy-start | bytes 442372
  12.3 25.4 %all-to-all-start.1 = ((bf16[64,2,1152]{2,1,0:T(2,128)(2,1)}), bf16[64,2,1152]{2,1,0:T(2,128)(2,1)S(1)}, u32[]{:S(2)}, u32[]{:S(2)}) async-start(bf16[64,2,1152]{2,1,0:T(2,128)(2,1)} %reshape.313), calls=%async_computation.1 | async-start | bytes 589824 | tf_op jit(solution)/shard_map/all_to_all | solution.py:82
  27.5 10.1 %copy-start.5 = (bf16[64,2,8,72]{3,2,1,0:T(8,128)(2,1)}, bf16[64,2,8,72]{3,2,1,0:T(8,128)(2,1)S(1)}, u32[]{:S(2)}) copy-start(bf16[64,2,8,72]{3,2,1,0:T(8,128)(2,1)S(1)} %reshape.281) | copy-start | bytes 442372
  27.8 9.8 %copy-start.7 = (bf16[64,2,8,72]{3,2,1,0:T(8,128)(2,1)}, bf16[64,2,8,72]{3,2,1,0:T(8,128)(2,1)S(1)}, u32[]{:S(2)}) copy-start(bf16[64,2,8,72]{3,2,1,0:T(8,128)(2,1)S(1)} %reshape.282) | copy-start | bytes 442372
  28.1 20.9 %copy-start.13 = (f32[2,8,64,64]{2,3,1,0:T(8,128)}, f32[2,8,64,64]{2,3,1,0:T(8,128)S(1)}, u32[]{:S(2)}) copy-start(f32[2,8,64,64]{2,3,1,0:T(8,128)S(1)} %get-tuple-element.25) | copy-start | bytes 786436
  28.4 0.7 copy-start.17
  37.6 18.9 %all-to-all-start = ((bf16[1,64,2,1152]{3,2,0,1:T(2,128)(2,1)}), bf16[1,64,2,1152]{3,2,0,1:T(2,128)(2,1)S(1)}, u32[]{:S(2)}, u32[]{:S(2)}) async-start(bf16[1,64,2,1152]{3,2,0,1:T(2,128)(2,1)} %copy.111), calls=%async_computation | async-start | bytes 589824 | tf_op jit(solution)/shard_map/all_to_all | solution.py:98
  45.0 13.5 %copy-start.21 = (bf16[1,1,128,576]{2,3,1,0:T(8,128)(2,1)S(1)}, bf16[1,1,128,576]{2,3,1,0:T(8,128)(2,1)}, u32[]{:S(2)}) copy-start(bf16[1,1,128,576]{2,3,1,0:T(8,128)(2,1)} %param.9) | copy-start | bytes 442372
  49.0 0.7 copy-start.18
  58.5 1.3 copy-start.25
  72.0 6.0 %copy-start.4 = (bf16[1,1,128,1152]{3,2,1,0:T(8,128)(2,1)S(1)}, bf16[1,1,128,1152]{3,2,1,0:T(8,128)(2,1)}, u32[]{:S(2)}) copy-start(bf16[1,1,128,1152]{3,2,1,0:T(8,128)(2,1)} %param.7) | copy-start | bytes 884740
  72.0 6.0 %copy-start.10 = (bf16[8,72,128]{2,1,0:T(8,128)(2,1)S(1)}, bf16[8,72,128]{2,1,0:T(8,128)(2,1)}, u32[]{:S(2)}) copy-start(bf16[8,72,128]{2,1,0:T(8,128)(2,1)} %convolution_convert_fusion.3) | copy-start | bytes 442372
  87.5 4.0 %copy-start.1 = (bf16[1152,64,2]{1,2,0:T(2,128)(2,1)S(1)}, bf16[1152,64,2]{1,2,0:T(2,128)(2,1)}, u32[]{:S(2)}) copy-start(bf16[1152,64,2]{1,2,0:T(2,128)(2,1)} %copy.128) | copy-start | bytes 884740
  87.5 4.0 %copy-start.9 = (bf16[4,144,64,2]{1,0,2,3:T(4,128)(2,1)S(1)}, bf16[4,144,64,2]{1,0,2,3:T(4,128)(2,1)}, u32[]{:S(2)}) copy-start(bf16[4,144,64,2]{1,0,2,3:T(4,128)(2,1)} %dot_general.122) | copy-start | bytes 442372
  91.4 1.0 copy-start.2
  91.4 2.3 slice-start
  91.5 2.4 slice-start.1
  196.7 9.0 %copy-start.14 = (f32[2,8,64,64]{2,3,1,0:T(8,128)S(1)}, f32[2,8,64,64]{2,3,1,0:T(8,128)}, u32[]{:S(2)}) copy-start(f32[2,8,64,64]{2,3,1,0:T(8,128)} %copy-done.13) | copy-start | bytes 786436
  196.7 10.6 %copy-start.8 = (bf16[64,2,8,72]{3,2,1,0:T(8,128)(2,1)S(1)}, bf16[64,2,8,72]{3,2,1,0:T(8,128)(2,1)}, u32[]{:S(2)}) copy-start(bf16[64,2,8,72]{3,2,1,0:T(8,128)(2,1)} %copy-done.7) | copy-start | bytes 442372
  198.8 8.3 %copy-start.15 = (f32[2,8,64,64]{2,3,1,0:T(8,128)S(1)}, f32[2,8,64,64]{2,3,1,0:T(8,128)}, u32[]{:S(2)}) copy-start(f32[2,8,64,64]{2,3,1,0:T(8,128)} %copy-done.13) | copy-start | bytes 786436
  198.8 10.1 %copy-start.6 = (bf16[64,2,8,72]{3,2,1,0:T(8,128)(2,1)S(1)}, bf16[64,2,8,72]{3,2,1,0:T(8,128)(2,1)}, u32[]{:S(2)}) copy-start(bf16[64,2,8,72]{3,2,1,0:T(8,128)(2,1)} %copy-done.5) | copy-start | bytes 442372
  198.8 11.7 %copy-start.11 = (bf16[8,72,128]{2,1,0:T(8,128)(2,1)S(1)}, bf16[8,72,128]{2,1,0:T(8,128)(2,1)}, u32[]{:S(2)}) copy-start(bf16[8,72,128]{2,1,0:T(8,128)(2,1)} %convolution_convert_fusion.3) | copy-start | bytes 442372
  198.8 40.3 %all-to-all-start.3 = ((bf16[64,2,5184]{2,1,0:T(2,128)(2,1)}), bf16[64,2,5184]{2,1,0:T(2,128)(2,1)}, u32[]{:S(2)}, u32[]{:S(2)}) async-start(bf16[64,2,5184]{2,1,0:T(2,128)(2,1)} %reshape.315), calls=%async_computation.3 | async-start | bytes 2686976 | tf_op jit(solution)/shard_map/all_to_all | solution.py:55
  205.8 7.2 %copy-start.12 = (f32[8,128,128]{1,2,0:T(8,128)S(1)}, f32[8,128,128]{1,2,0:T(8,128)}, u32[]{:S(2)}) copy-start(f32[8,128,128]{1,2,0:T(8,128)} %get-tuple-element.27) | copy-start | bytes 1572868
  205.8 7.2 %copy-start.24 = (bf16[128,576]{0,1:T(8,128)(2,1)S(1)}, bf16[128,576]{0,1:T(8,128)(2,1)}, u32[]{:S(2)}) copy-start(bf16[128,576]{0,1:T(8,128)(2,1)} %copy-done.23) | copy-start | bytes 442372
  205.8 7.2 %copy-start.26 = (bf16[128,576]{0,1:T(8,128)(2,1)S(1)}, bf16[128,576]{0,1:T(8,128)(2,1)}, u32[]{:S(2)}) copy-start(bf16[128,576]{0,1:T(8,128)(2,1)} %copy-done.25) | copy-start | bytes 442372
  207.3 7.1 %copy-start.22 = (bf16[1,1,128,576]{2,3,1,0:T(8,128)(2,1)S(1)}, bf16[1,1,128,576]{2,3,1,0:T(8,128)(2,1)}, u32[]{:S(2)}) copy-start(bf16[1,1,128,576]{2,3,1,0:T(8,128)(2,1)} %param.9) | copy-start | bytes 442372

commit v2 on v0

v2 whole, which is shorter than its diff:
```python
import functools

import jax
import jax.numpy as jnp
import numpy as np
from jax import lax
from jax.experimental import pallas as pl
from jax.experimental.pallas import tpu as pltpu
from jax.sharding import PartitionSpec as P

HEADS = 8
HEAD_DIM = 72
WIDTH = 1152
INNER = 576
TOKENS = 128
SCORE_SCALE = HEAD_DIM ** (-0.5)
ROW_BLOCK = 144
LANES = 384
SHARE_ROWS = 32
CUT = 80
F32 = jnp.float32
BF16 = jnp.bfloat16
MESH = pl.DeviceIdType.MESH


def one_hot(source, size):
    table = np.zeros((len(source), size), np.float32)
    for row, at in enumerate(source):
        if at >= 0:
            table[row, at] = 1.0
    return table


def make_tables():
    def natural(y_lo, z, x, p):
        return 2 * (y_lo * 32 + z * 4 + x) + p

    to_z = [natural(y, z, x, p) for z in range(8) for y in range(2) for x in range(4) for p in range(2)]
    to_plane = [z * 16 + q * 2 + p for q in range(8) for z in range(8) for p in range(2)]
    to_natural = [
        (y * 4 + x) * 16 + z * 2 + p for y in range(2) for z in range(8) for x in range(4) for p in range(2)
    ]
    token_moves = np.stack([one_hot(order, TOKENS) for order in (to_z, to_plane, to_natural)])
    feature_moves = np.stack(
        [
            one_hot(
                [y * 64 + z * 72 + x * 18 + r for x in range(4) for z in range(8) for r in range(18)], 640
            )
            for y in range(2)
        ]
    )
    picks = np.zeros((2, 2, 2, INNER, LANES), np.float32)
    for core in range(2):
        for matrix in range(2):
            for y_hi in range(2):
                for column in range(144):
                    picks[core, matrix, y_hi, (2 * y_hi + core) * 144 + column, matrix * 144 + column] = 1.0
    share_moves = one_hot([z * 18 + r if r < 18 else -1 for z in range(8) for r in range(SHARE_ROWS)], ROW_BLOCK)
    return [jnp.asarray(table, BF16) for table in (token_moves, feature_moves, picks, share_moves)]


def dot(left, right):
    return jnp.dot(left, right, preferred_element_type=F32)


def dot_nt(left, right):
    return lax.dot_general(left, right, (((1,), (1,)), ((), ())), preferred_element_type=F32)


def dot_tn(left, right):
    return lax.dot_general(left, right, (((0,), (0,)), ((), ())), preferred_element_type=F32)


def head_window(head):
    start = head * HEAD_DIM // 128 * 128
    stop = min(-(-(head * HEAD_DIM + HEAD_DIM) // 128) * 128, INNER)
    return start, stop


def head_mask(head):
    start, stop = head_window(head)
    lane = lax.broadcasted_iota(jnp.int32, (TOKENS, stop - start), 1) + start
    return (lane >= head * HEAD_DIM) & (lane < (head + 1) * HEAD_DIM)


def window(ref, head):
    start, stop = head_window(head)
    return ref[:, start:stop]


def masked_window(ref, head):
    return jnp.where(head_mask(head), window(ref, head).astype(F32), 0.0).astype(BF16)


def join_heads(parts):
    tiles = [None] * 5
    for head, part in enumerate(parts):
        start, stop = head_window(head)
        part = jnp.where(head_mask(head), part, 0.0)
        for at in range(start, stop, 128):
            piece = part[:, at - start : min(at - start + 128, stop - start)]
            tiles[at // 128] = piece if tiles[at // 128] is None else tiles[at // 128] + piece
    return jnp.concatenate(tiles, axis=1)


def softmax_heads(queries, key_rows, chance_ref, bias):
    for head in range(HEADS):
        scores = dot_nt(masked_window(queries, head), window(key_rows, head)) * SCORE_SCALE
        if bias is not None:
            scores = scores + bias
        powers = jnp.exp(scores - jnp.max(scores, axis=1, keepdims=True))
        chance_ref[head] = powers / jnp.sum(powers, axis=1, keepdims=True)


def attend(chance_ref, values):
    return join_heads([dot(chance_ref[h].astype(BF16), window(values, h)) for h in range(HEADS)])


def attend_values_back(chance_ref, out_grad):
    return join_heads([dot_tn(chance_ref[h].astype(BF16), window(out_grad, h)) for h in range(HEADS)])


def attend_scores_back(chance_ref, queries, key_rows, values, out_grad):
    query_parts, key_parts = [], []
    for head in range(HEADS):
        chance = chance_ref[head]
        chance_grad = dot_nt(masked_window(out_grad, head), window(values, head))
        centre = jnp.sum(chance * chance_grad, axis=1, keepdims=True)
        score_grad = (chance * (chance_grad - centre)).astype(BF16)
        query_parts.append(dot(score_grad, window(key_rows, head)))
        key_parts.append(dot_tn(score_grad, window(queries, head)))
    return join_heads(query_parts) * SCORE_SCALE, join_heads(key_parts) * SCORE_SCALE


def kernel(
    grad_scale,
    block_hbm, sq_hbm, sk_hbm, cot_hbm, tq_hbm, tk_hbm, weights_hbm,
    token_moves_hbm, feature_moves_hbm, picks_hbm, share_moves_hbm,
    input_grad, sq_grad, sk_grad, tq_grad, tk_grad, weight_grads,
    block, sq, sk, cot, tq, tk, weights, token_moves, feature_moves, picks, share_moves,
    chance_s, chance_t, value_s, value_t, attended_s, attended_t, at_grad, as_grad, vt_grad, vs_grad,
    mixed, mixed_grad,
    out_z, in_z, out_plane, in_plane,
    factors, picked, picked_out, sums, arrived, sums_two, arrived_two, shares, shares_in,
    load_sem, z_send, z_recv, plane_send, plane_recv, factor_send, factor_recv, picked_send, picked_recv,
    ring_send, ring_recv, ring_two_send, ring_two_recv, share_send, share_recv,
):
    dp, seq = lax.axis_index("dp"), lax.axis_index("seq")
    y_hi, core = dp // 2, dp % 2
    y_lo, z, x = seq // 32, (seq // 4) % 8, seq % 4
    y = y_hi * 2 + y_lo
    q = y_lo * 4 + x

    def device(y_hi_at=y_hi, core_at=core, y_lo_at=y_lo, z_at=z, x_at=x):
        return (y_hi_at * 2 + core_at, y_lo_at * 32 + z_at * 4 + x_at)

    def along_z(step):
        return device(z_at=(z + step) % 8)

    def in_the_plane(step):
        to = (q + step) % 8
        return device(y_lo_at=to // 4, x_at=to % 4)

    def along_x(step):
        return device(x_at=(x + step) % 4)

    def along_y(step):
        to = (y + step) % 4
        return device(y_hi_at=to // 2, y_lo_at=to % 2)

    sibling = device(core_at=1 - core)

    loads = []
    for number, (source, target) in enumerate(
        [
            (tq_hbm, tq), (tk_hbm, tk), (cot_hbm, cot), (weights_hbm.at[3], weights.at[3]),
            (weights_hbm.at[2], weights.at[2]), (token_moves_hbm, token_moves), (block_hbm, block),
            (weights_hbm.at[0], weights.at[0]), (sq_hbm, sq), (sk_hbm, sk), (weights_hbm.at[1], weights.at[1]),
            (feature_moves_hbm, feature_moves), (picks_hbm, picks), (share_moves_hbm, share_moves),
        ]
    ):
        copy = pltpu.make_async_copy(source, target, load_sem.at[number])
        copy.start()
        loads.append(copy)

    barrier = pltpu.get_barrier_semaphore()
    greeted = [along_z(step) for step in range(1, 8)] + [in_the_plane(step) for step in range(1, 8)]
    greeted += [device(y_hi_at=1 - y_hi, y_lo_at=1 - y_lo), sibling]
    for peer in greeted:
        pl.semaphore_signal(barrier, inc=1, device_id=peer, device_id_type=MESH)

    sent = []

    def send(source, target, send_sem, recv_sem, peer):
        copy = pltpu.make_async_remote_copy(
            src_ref=source, dst_ref=target, send_sem=send_sem, recv_sem=recv_sem,
            device_id=peer, device_id_type=MESH,
        )
        copy.start()
        sent.append(copy)
        return copy

    def move_tokens(number, rows):
        return dot(token_moves[number], rows).astype(BF16)

    def start_z(item):
        copies = []
        for step in range(1, 8):
            to = (z + step) % 8
            copies.append(
                send(
                    out_z.at[item, pl.ds(to * 16, 16)], in_z.at[item, pl.ds(z * 16, 16)],
                    z_send.at[item, step - 1], z_recv.at[item, step - 1], along_z(step),
                )
            )
        own = pl.ds(pl.multiple_of(z * 16, 16), 16)
        in_z[item, own, :] = out_z[item, own, :]
        return copies

    def start_plane(item):
        copies = []
        for step in range(1, 8):
            to = (q + step) % 8
            copies.append(
                send(
                    out_plane.at[item, pl.ds(to * 16, 16)], in_plane.at[item, pl.ds(q * 16, 16)],
                    plane_send.at[item, step - 1], plane_recv.at[item, step - 1], in_the_plane(step),
                )
            )
        own = pl.ds(pl.multiple_of(q * 16, 16), 16)
        in_plane[item, own, :] = out_plane[item, own, :]
        return copies

    def arrive(copies):
        for copy in copies:
            copy.wait_recv()

    def start_features(number, rows_ref):
        for half in range(2):
            factors[number, half * INNER : (half + 1) * INNER, 0:TOKENS] = dot_nt(
                feature_moves[half], rows_ref[:, half * 512 : half * 512 + 640]
            ).astype(BF16)
        return send(
            factors.at[number, :, 0:TOKENS], factors.at[number, :, TOKENS : 2 * TOKENS],
            factor_send.at[number], factor_recv.at[number], sibling,
        )

    def start_columns(number, rows):
        for side in range(2):
            picked[number, side, 0:TOKENS, :] = dot(rows, picks[core, number % 2, side]).astype(BF16)
            picked_out[number, side] = dot(rows, picks[1 - core, number % 2, side]).astype(BF16)
        return send(
            picked_out.at[number], picked.at[number, :, TOKENS : 2 * TOKENS],
            picked_send.at[number], picked_recv.at[number], sibling,
        )

    def block_sum(pair, side, y_lo_at, x_at):
        rows = pl.ds(pl.multiple_of((y_lo_at * 4 + x_at) * ROW_BLOCK, 16), ROW_BLOCK)
        total = dot(factors[2 * pair, rows, :], picked[2 * pair, side])
        total += dot(factors[2 * pair + 1, rows, :], picked[2 * pair + 1, side])
        sums[pair, side, y_lo_at, x_at] = total.astype(BF16)

    def piece(pair, to, half):
        if pair == 0:
            return sums.at[0, half, :, to]
        return sums.at[1, to // 2, to % 2, 2 * half : 2 * half + 2]

    def make_pieces(pair, to):
        if pair == 0:
            for side in range(2):
                for y_lo_at in range(2):
                    block_sum(0, side, y_lo_at, to)
        else:
            for x_at in range(4):
                block_sum(1, to // 2, to % 2, x_at)

    places = (x, y)
    rings = (along_x, along_y)

    def ring_copy(pair, slot, source):
        peer = rings[pair](1 if slot % 2 == 0 else -1 + 4)
        return send(source, arrived.at[pair, slot], ring_send.at[pair, slot], ring_recv.at[pair, slot], peer)

    def first_ring(pair):
        place = places[pair]
        after, across, before = (place + 1) % 4, (place + 2) % 4, (place + 3) % 4
        copies = {}
        make_pieces(pair, across)
        copies[0] = ring_copy(pair, 0, piece(pair, across, 0))
        copies[1] = ring_copy(pair, 1, piece(pair, across, 1))
        make_pieces(pair, after)
        copies[2] = ring_copy(pair, 2, piece(pair, after, 1))
        make_pieces(pair, before)
        copies[3] = ring_copy(pair, 3, piece(pair, before, 0))
        make_pieces(pair, place)
        return copies

    def first_relay(pair, copies):
        place = places[pair]
        after, before = (place + 1) % 4, (place + 3) % 4
        for slot, to, half in ((0, after, 0), (1, before, 1)):
            copies[slot].wait_recv()
            ref = piece(pair, to, half)
            ref[...] = (ref[...].astype(F32) + arrived[pair, slot].astype(F32)).astype(BF16)
            copies[slot + 4] = ring_copy(pair, slot + 4, ref)

    def first_end(pair, copies):
        for half, slots in ((0, (3, 4)), (1, (2, 5))):
            total = piece(pair, places[pair], half)[...].astype(F32)
            for slot in slots:
                copies[slot].wait_recv()
                total += arrived[pair, slot].astype(F32)
            sums_two[pair, 2 * half : 2 * half + 2] = total.astype(BF16)

    def part_two(pair, to, half):
        return sums_two.at[pair, to, 0:CUT] if half == 0 else sums_two.at[pair, to, CUT:ROW_BLOCK]

    def slot_two(pair, slot, half):
        return arrived_two.at[pair, slot, 0 : (CUT if half == 0 else ROW_BLOCK - CUT)]

    slot_half = (0, 1, 1, 0, 0, 1)

    def ring_two_copy(pair, slot, source):
        peer = rings[1 - pair](1 if slot % 2 == 0 else -1 + 4)
        return send(
            source, slot_two(pair, slot, slot_half[slot]),
            ring_two_send.at[pair, slot], ring_two_recv.at[pair, slot], peer,
        )

    def second_ring(pair):
        place = places[1 - pair]
        after, across, before = (place + 1) % 4, (place + 2) % 4, (place + 3) % 4
        copies = {}
        copies[0] = ring_two_copy(pair, 0, part_two(pair, across, 0))
        copies[1] = ring_two_copy(pair, 1, part_two(pair, across, 1))
        copies[2] = ring_two_copy(pair, 2, part_two(pair, after, 1))
        copies[3] = ring_two_copy(pair, 3, part_two(pair, before, 0))
        return copies

    def second_relay(pair, copies):
        place = places[1 - pair]
        after, before = (place + 1) % 4, (place + 3) % 4
        for slot, to, half in ((0, after, 0), (1, before, 1)):
            copies[slot].wait_recv()
            ref = part_two(pair, to, half)
            ref[...] = (ref[...].astype(F32) + slot_two(pair, slot, half)[...].astype(F32)).astype(BF16)
            copies[slot + 4] = ring_two_copy(pair, slot + 4, ref)

    def second_end(pair, copies):
        place = places[1 - pair]
        halves = []
        for half, slots in ((0, (3, 4)), (1, (2, 5))):
            total = part_two(pair, place, half)[...].astype(F32)
            for slot in slots:
                copies[slot].wait_recv()
                total += slot_two(pair, slot, half)[...].astype(F32)
            halves.append(total.astype(BF16))
        shares[pair] = dot(share_moves[...], jnp.concatenate(halves, axis=0)).astype(BF16)
        last = []
        for step in range(1, 8):
            to = (z + step) % 8
            last.append(
                send(
                    shares.at[pair, pl.ds(to * SHARE_ROWS, SHARE_ROWS)], shares_in.at[pair, step - 1],
                    share_send.at[pair, step - 1], share_recv.at[pair, step - 1], along_z(step),
                )
            )
        return last

    def finish(pair, copies):
        own = pl.ds(pl.multiple_of(z * SHARE_ROWS, SHARE_ROWS), SHARE_ROWS)
        total = shares[pair, own, :].astype(F32)
        for step in range(1, 8):
            copies[step - 1].wait_recv()
            total += shares_in[pair, step - 1].astype(F32)
        total = total * grad_scale
        weight_grads[2 * pair] = total[0:18, 0:144]
        weight_grads[2 * pair + 1] = total[0:18, 144:288]

    loads[0].wait()
    loads[1].wait()
    row_patch = lax.broadcasted_iota(jnp.int32, (TOKENS, TOKENS), 0) % 2
    column_patch = lax.broadcasted_iota(jnp.int32, (TOKENS, TOKENS), 1) % 2
    softmax_heads(tq, tk, chance_t, jnp.where(row_patch == column_patch, 0.0, -1e30))
    loads[2].wait()
    loads[3].wait()
    at_grad[...] = dot(cot[...], weights[3]).astype(BF16)
    vt_grad[...] = attend_values_back(chance_t, at_grad).astype(BF16)
    loads[4].wait()
    loads[5].wait()
    out_z[1] = move_tokens(0, (cot[...].astype(F32) + dot_nt(vt_grad[...], weights[2])).astype(BF16))
    pl.semaphore_wait(barrier, len(greeted))
    grad_z = start_z(1)

    for number in (6, 7, 8, 9, 10):
        loads[number].wait()
    value_s[...] = dot(block[...], weights[0]).astype(BF16)
    softmax_heads(sq, sk, chance_s, None)
    attended_s[...] = attend(chance_s, value_s).astype(BF16)
    out_z[0] = move_tokens(0, (block[...].astype(F32) + dot_nt(attended_s[...], weights[1])).astype(BF16))
    mixed_z = start_z(0)

    for number in (11, 12, 13):
        loads[number].wait()
    arrive(grad_z)
    out_plane[1] = move_tokens(1, in_z[1])
    grad_plane = start_plane(1)
    feature_copies, column_copies = {}, {}
    feature_copies[0] = start_features(0, block)
    feature_copies[3] = start_features(3, cot)
    column_copies[1] = start_columns(1, attended_s[...])
    column_copies[2] = start_columns(2, vt_grad[...])
    arrive(mixed_z)
    out_plane[0] = move_tokens(1, in_z[0])
    mixed_plane = start_plane(0)

    arrive(grad_plane)
    mixed_grad[...] = move_tokens(2, in_plane[1])
    feature_copies[1] = start_features(1, mixed_grad)
    as_grad[...] = dot(mixed_grad[...], weights[1]).astype(BF16)
    vs_grad[...] = attend_values_back(chance_s, as_grad).astype(BF16)
    column_copies[0] = start_columns(0, vs_grad[...])

    arrive(mixed_plane)
    mixed[...] = move_tokens(2, in_plane[0])
    feature_copies[2] = start_features(2, mixed)
    value_t[...] = dot(mixed[...], weights[2]).astype(BF16)
    attended_t[...] = attend(chance_t, value_t).astype(BF16)
    column_copies[3] = start_columns(3, attended_t[...])

    arrive([feature_copies[0], feature_copies[1], column_copies[0], column_copies[1]])
    first_s = first_ring(0)
    arrive([feature_copies[2], feature_copies[3], column_copies[2], column_copies[3]])
    first_t = first_ring(1)
    first_relay(0, first_s)
    query_part, key_part = attend_scores_back(chance_s, sq, sk, value_s, as_grad)
    sq_grad[...] = query_part.astype(BF16)
    sk_grad[...] = key_part.astype(BF16)
    first_relay(1, first_t)
    input_grad[...] = (mixed_grad[...].astype(F32) + dot_nt(vs_grad[...], weights[0])).astype(BF16)
    query_part, key_part = attend_scores_back(chance_t, tq, tk, value_t, at_grad)
    tq_grad[...] = query_part.astype(BF16)
    tk_grad[...] = key_part.astype(BF16)

    first_end(0, first_s)
    second_s = second_ring(0)
    first_end(1, first_t)
    second_t = second_ring(1)
    second_relay(0, second_s)
    second_relay(1, second_t)
    last_s = second_end(0, second_s)
    last_t = second_end(1, second_t)
    finish(0, last_s)
    finish(1, last_t)
    for copy in sent:
        copy.wait_send()


def body(
    block_input, spatial_queries, spatial_keys, cotangent, temporal_queries, temporal_keys, weights
):
    grad_scale = float(4 * 64 * 128) ** (-0.5)
    tables = make_tables()
    arrays = [
        block_input.reshape(TOKENS, WIDTH),
        spatial_queries.reshape(TOKENS, INNER),
        spatial_keys.reshape(TOKENS, INNER),
        cotangent.reshape(TOKENS, WIDTH),
        temporal_queries.reshape(TOKENS, INNER),
        temporal_keys.reshape(TOKENS, INNER),
        weights,
    ] + tables
    wide, narrow = (TOKENS, WIDTH), (TOKENS, INNER)
    chances = pltpu.VMEM((HEADS, TOKENS, TOKENS), F32)
    dma = pltpu.SemaphoreType.DMA
    scratch = [pltpu.VMEM(array.shape, BF16) for array in arrays]
    scratch += [chances, chances] + [pltpu.VMEM(narrow, BF16)] * 8
    scratch += [pltpu.VMEM(wide, BF16)] * 2 + [pltpu.VMEM((2,) + wide, BF16)] * 4
    scratch += [
        pltpu.VMEM((4, WIDTH, 2 * TOKENS), BF16),
        pltpu.VMEM((4, 2, 2 * TOKENS, LANES), BF16),
        pltpu.VMEM((4, 2, TOKENS, LANES), BF16),
        pltpu.VMEM((2, 2, 2, 4, ROW_BLOCK, LANES), BF16),
        pltpu.VMEM((2, 6, 2, ROW_BLOCK, LANES), BF16),
        pltpu.VMEM((2, 4, ROW_BLOCK, LANES), BF16),
        pltpu.VMEM((2, 6, CUT, LANES), BF16),
        pltpu.VMEM((2, 8 * SHARE_ROWS, LANES), BF16),
        pltpu.VMEM((2, 7, SHARE_ROWS, LANES), BF16),
    ]
    scratch += [dma((14,))] + [dma((2, 7))] * 4 + [dma((4,))] * 4 + [dma((2, 6))] * 4 + [dma((2, 7))] * 2
    bf16_out = [jax.ShapeDtypeStruct(wide, BF16)] + [jax.ShapeDtypeStruct(narrow, BF16)] * 4
    input_grad, sq_grad, sk_grad, tq_grad, tk_grad, weight_grads = pl.pallas_call(
        functools.partial(kernel, grad_scale),
        out_shape=bf16_out + [jax.ShapeDtypeStruct((4, 18, 144), F32)],
        in_specs=[pl.BlockSpec(memory_space=pl.ANY)] * len(arrays),
        out_specs=[pl.BlockSpec(memory_space=pltpu.VMEM)] * 6,
        scratch_shapes=scratch,
        compiler_params=pltpu.CompilerParams(
            collective_id=0, has_side_effects=True, vmem_limit_bytes=56 * 2**20
        ),
        name="block_backward",
    )(*arrays)
    return (
        input_grad.reshape(block_input.shape),
        sq_grad.reshape(spatial_queries.shape),
        sk_grad.reshape(spatial_keys.shape),
        tq_grad.reshape(temporal_queries.shape),
        tk_grad.reshape(temporal_keys.shape),
        weight_grads,
    )


def solution(mesh):
    placed = (
        P("dp", "seq", None, None),
        P("dp", "seq", None, None),
        P("dp", "seq", None, None),
        P("dp", None, "seq", None),
        P("dp", None, "seq", None),
        P("dp", None, "seq", None),
        P(),
    )
    return jax.shard_map(
        body,
        mesh=mesh,
        in_specs=placed,
        out_specs=(
            P("dp", "seq", None, None),
            P("dp", "seq", None, None),
            P("dp", "seq", None, None),
            P("dp", None, "seq", None),
            P("dp", None, "seq", None),
            P(None, "seq", "dp"),
        ),
        check_vma=False,
    )
```

time: 570 us -> 96.3 us (0.17)
  blocking collectives: 373 us -> 0 us
  Pallas kernels: 0 us -> 67.6 us
  waiting for transfers between devices: 62.3 us -> 0 us
  local copies, waits for them, and re-layouts: 56.8 us -> 27.1 us
  matrix products: 27.4 us -> 0 us
  starting transfers between devices: 22.5 us -> 0 us
  between operations: 15.2 us -> 0.65 us
  other arithmetic: 10.6 us -> 0 us
    unnamed x1 -> x0, blocking collectives: 373 us -> none
    pallas_call x0 -> x1, Pallas kernels: none -> 67.6 us  [body(): pl.pallas_call(functools.partial(kernel, grad_scale), out_shape=bf16_out...]
    unnamed x4 -> x0, waiting for transfers between devices: 54.9 us -> none
    dot_general x21 -> x0, matrix products: 26.7 us -> none  [project(): jnp.einsum(einsum_form, left_side, right_side, preferred_element_type=jnp...]
    mul x2 -> x0, local copies, waits for them, and re-layouts: 22.8 us -> none  [the longest x1 11.4 us: body(): jnp.stack([value_weight_sp, out_weight_sp]) * grad_scale]
    all_to_all x2 -> x0, starting transfers between devices: 22 us -> none  [the longest x1 13 us: body(): lax.all_to_all(mixed_tm_grad, 'seq', split_axis=1, concat_axis=2, tiled=T...]
    reshape x0 -> x5, local copies, waits for them, and re-layouts: none -> 8.51 us  [the longest x1 1.78 us: body(): cotangent.reshape(TOKENS, WIDTH)]
    all_to_all x2 -> x0, waiting for transfers between devices: 7.45 us -> none  [the longest x1 5.16 us: body(): lax.all_to_all(mixed, 'seq', split_axis=2, concat_axis=1, tiled=True)]
  transfers between devices with their start and end apart: 4 -> 0, of which waited for: 4 -> 0; matrix products, arithmetic and copies ran while one was open for 5% -> 0% of each run, Pallas kernels for 0% -> 0%
where the time goes in v2:
time: 96.3 us; the launch traced here: 95.3 us
  Pallas kernels  67.6 us (70%)
  local copies, waits for them, and re-layouts  27.1 us (28%)
    pallas_call x1, Pallas kernels, body(): pl.pallas_call(functools.partial(kernel, grad_scale), out_shape=bf16_out...  67.6 us
    unnamed x7, local copies, waits for them, and re-layouts  18.6 us

profile of v2, /device:TPU:4, one launch (start us, length us, event | category | flops | bytes accessed | tf_op | source)
XLA Modules:
  0.0 95.3 jit_solution(7913537229495105135)
XLA Ops:
  0.6 1.7 %copy.23 = bf16[1,1,128,576]{3,2,1,0:T(8,128)(2,1)} copy(bf16[1,1,128,576]{2,3,1,0:T(8,128)(2,1)} %param.12) | data formatting | bytes 294912 | tf_op args[1]
  2.3 1.7 %copy.24 = bf16[1,1,128,576]{3,2,1,0:T(8,128)(2,1)} copy(bf16[1,1,128,576]{2,3,1,0:T(8,128)(2,1)} %param.13) | data formatting | bytes 294912 | tf_op args[2]
  4.1 1.7 %reshape.49.tq_hbm = bf16[128,576]{1,0:T(8,128)(2,1)} reshape(bf16[1,64,2,576]{3,2,1,0:T(2,128)(2,1)} %param.15) | data formatting | bytes 294912 | tf_op jit(solution)/shard_map/reshape | solution.py:469
  5.8 1.7 %reshape.50.tk_hbm = bf16[128,576]{1,0:T(8,128)(2,1)} reshape(bf16[1,64,2,576]{3,2,1,0:T(2,128)(2,1)} %param.16) | data formatting | bytes 294912 | tf_op jit(solution)/shard_map/reshape | solution.py:470
  7.5 1.8 %reshape.48.cot_hbm = bf16[128,1152]{1,0:T(8,128)(2,1)} reshape(bf16[1,64,2,1152]{3,2,1,0:T(2,128)(2,1)} %param.14) | data formatting | bytes 589824 | tf_op jit(solution)/shard_map/reshape | solution.py:468
  9.3 8.6 %copy.25.weights_hbm = bf16[4,1152,576]{2,1,0:T(8,128)(2,1)} copy(bf16[4,1152,576]{1,2,0:T(8,128)(2,1)} %param.17) | data formatting | bytes 10616832 | tf_op args[6]
  17.8 67.6 %block_backward.1 = (bf16[128,1152]{1,0:T(8,128)(2,1)}, bf16[128,576]{1,0:T(8,128)(2,1)}, bf16[128,576]{1,0:T(8,128)(2,1)}, bf16[128,576]{1,0:T(8,128)(2,1)}, bf...) custom-call(bf16[128,1152]{1,0:T(8,128)(2,1)} %bitcast.8, bf16[128,576]{1,0:T(8,128)(2,1)} %bitcast.6, ...), custom_call_target="tpu_custom_call" | custom-call | tf_op jit(solution)/shard_map/block_backward/pallas_call | solution.py:492
  85.4 1.7 %copy.26 = bf16[1,1,128,576]{2,3,1,0:T(8,128)(2,1)} copy(bf16[1,1,128,576]{3,2,1,0:T(8,128)(2,1)} %bitcast.11) | data formatting | bytes 294912
  87.1 1.6 %copy.28 = f32[4,18,144]{2,0,1:T(4,128)} copy(f32[4,18,144]{2,1,0:T(8,128)} %get-tuple-element.29) | data formatting | bytes 82944
  88.6 1.7 %copy.27 = bf16[1,1,128,576]{2,3,1,0:T(8,128)(2,1)} copy(bf16[1,1,128,576]{3,2,1,0:T(8,128)(2,1)} %bitcast.10) | data formatting | bytes 294912
  90.3 1.7 %reshape.54 = bf16[1,64,2,576]{3,2,1,0:T(2,128)(2,1)} reshape(bf16[128,576]{1,0:T(8,128)(2,1)} %get-tuple-element.15) | data formatting | bytes 294912 | tf_op jit(solution)/shard_map/reshape | solution.py:507
  92.0 1.7 %reshape.55 = bf16[1,64,2,576]{3,2,1,0:T(2,128)(2,1)} reshape(bf16[128,576]{1,0:T(8,128)(2,1)} %get-tuple-element.16) | data formatting | bytes 294912 | tf_op jit(solution)/shard_map/reshape | solution.py:508
  93.6 1.7 %copy.30 = bf16[1,1,128,1152]{3,2,1,0:T(8,128)(2,1)} copy(bf16[1,1,128,1152]{3,2,1,0:T(8,128)(2,1)} %bitcast.9) | data formatting | bytes 589824

commit v3 on v2

--- a/solution.py
+++ b/solution.py
@@ -13,6 +13,7 @@
 WIDTH = 1152
 INNER = 576
 TOKENS = 128
+FRAMES = 64
 SCORE_SCALE = HEAD_DIM ** (-0.5)
 ROW_BLOCK = 144
 LANES = 384
@@ -137,7 +138,8 @@
     block_hbm, sq_hbm, sk_hbm, cot_hbm, tq_hbm, tk_hbm, weights_hbm,
     token_moves_hbm, feature_moves_hbm, picks_hbm, share_moves_hbm,
     input_grad, sq_grad, sk_grad, tq_grad, tk_grad, weight_grads,
-    block, sq, sk, cot, tq, tk, weights, token_moves, feature_moves, picks, share_moves,
+    block, sq_turned, sk_turned, cot_pairs, tq_pairs, tk_pairs, weights, token_moves, feature_moves, picks, share_moves,
+    sq, sk, cot, tq, tk, rows_wide, rows_one, rows_two,
     chance_s, chance_t, value_s, value_t, attended_s, attended_t, at_grad, as_grad, vt_grad, vs_grad,
     mixed, mixed_grad,
     out_z, in_z, out_plane, in_plane,
@@ -173,9 +175,9 @@
     loads = []
     for number, (source, target) in enumerate(
         [
-            (tq_hbm, tq), (tk_hbm, tk), (cot_hbm, cot), (weights_hbm.at[3], weights.at[3]),
+            (tq_hbm, tq_pairs), (tk_hbm, tk_pairs), (cot_hbm, cot_pairs), (weights_hbm.at[3], weights.at[3]),
             (weights_hbm.at[2], weights.at[2]), (token_moves_hbm, token_moves), (block_hbm, block),
-            (weights_hbm.at[0], weights.at[0]), (sq_hbm, sq), (sk_hbm, sk), (weights_hbm.at[1], weights.at[1]),
+            (weights_hbm.at[0], weights.at[0]), (sq_hbm, sq_turned), (sk_hbm, sk_turned), (weights_hbm.at[1], weights.at[1]),
             (feature_moves_hbm, feature_moves), (picks_hbm, picks), (share_moves_hbm, share_moves),
         ]
     ):
@@ -374,30 +376,44 @@
             copies[step - 1].wait_recv()
             total += shares_in[pair, step - 1].astype(F32)
         total = total * grad_scale
-        weight_grads[2 * pair] = total[0:18, 0:144]
-        weight_grads[2 * pair + 1] = total[0:18, 144:288]
+        weight_grads[:, 2 * pair, :] = total[0:18, 0:144]
+        weight_grads[:, 2 * pair + 1, :] = total[0:18, 144:288]
+
+    def join_pairs(pairs, rows):
+        for frame in range(FRAMES):
+            rows[2 * frame : 2 * frame + 2, :] = pairs[frame].astype(F32)
+        return rows[...].astype(BF16)
+
+    def split_pairs(rows, pairs):
+        for frame in range(FRAMES):
+            pairs[frame] = rows[2 * frame : 2 * frame + 2, :].astype(BF16)
 
     loads[0].wait()
     loads[1].wait()
+    tq[...] = join_pairs(tq_pairs, rows_one)
+    tk[...] = join_pairs(tk_pairs, rows_two)
     row_patch = lax.broadcasted_iota(jnp.int32, (TOKENS, TOKENS), 0) % 2
     column_patch = lax.broadcasted_iota(jnp.int32, (TOKENS, TOKENS), 1) % 2
     softmax_heads(tq, tk, chance_t, jnp.where(row_patch == column_patch, 0.0, -1e30))
     loads[2].wait()
     loads[3].wait()
-    at_grad[...] = dot(cot[...], weights[3]).astype(BF16)
+    cot[...] = join_pairs(cot_pairs, rows_wide)
+    at_grad[...] = dot_nt(cot[...], weights[3]).astype(BF16)
     vt_grad[...] = attend_values_back(chance_t, at_grad).astype(BF16)
     loads[4].wait()
     loads[5].wait()
-    out_z[1] = move_tokens(0, (cot[...].astype(F32) + dot_nt(vt_grad[...], weights[2])).astype(BF16))
+    out_z[1] = move_tokens(0, (cot[...].astype(F32) + dot(vt_grad[...], weights[2])).astype(BF16))
     pl.semaphore_wait(barrier, len(greeted))
     grad_z = start_z(1)
 
     for number in (6, 7, 8, 9, 10):
         loads[number].wait()
-    value_s[...] = dot(block[...], weights[0]).astype(BF16)
+    sq[...] = sq_turned[...].T
+    sk[...] = sk_turned[...].T
+    value_s[...] = dot_nt(block[...], weights[0]).astype(BF16)
     softmax_heads(sq, sk, chance_s, None)
     attended_s[...] = attend(chance_s, value_s).astype(BF16)
-    out_z[0] = move_tokens(0, (block[...].astype(F32) + dot_nt(attended_s[...], weights[1])).astype(BF16))
+    out_z[0] = move_tokens(0, (block[...].astype(F32) + dot(attended_s[...], weights[1])).astype(BF16))
     mixed_z = start_z(0)
 
     for number in (11, 12, 13):
@@ -417,14 +433,14 @@
     arrive(grad_plane)
     mixed_grad[...] = move_tokens(2, in_plane[1])
     feature_copies[1] = start_features(1, mixed_grad)
-    as_grad[...] = dot(mixed_grad[...], weights[1]).astype(BF16)
+    as_grad[...] = dot_nt(mixed_grad[...], weights[1]).astype(BF16)
     vs_grad[...] = attend_values_back(chance_s, as_grad).astype(BF16)
     column_copies[0] = start_columns(0, vs_grad[...])
 
     arrive(mixed_plane)
     mixed[...] = move_tokens(2, in_plane[0])
     feature_copies[2] = start_features(2, mixed)
-    value_t[...] = dot(mixed[...], weights[2]).astype(BF16)
+    value_t[...] = dot_nt(mixed[...], weights[2]).astype(BF16)
     attended_t[...] = attend(chance_t, value_t).astype(BF16)
     column_copies[3] = start_columns(3, attended_t[...])
 
@@ -434,13 +450,15 @@
     first_t = first_ring(1)
     first_relay(0, first_s)
     query_part, key_part = attend_scores_back(chance_s, sq, sk, value_s, as_grad)
-    sq_grad[...] = query_part.astype(BF16)
-    sk_grad[...] = key_part.astype(BF16)
+    sq_grad[...] = query_part.astype(BF16).T
+    sk_grad[...] = key_part.astype(BF16).T
     first_relay(1, first_t)
-    input_grad[...] = (mixed_grad[...].astype(F32) + dot_nt(vs_grad[...], weights[0])).astype(BF16)
+    input_grad[...] = (mixed_grad[...].astype(F32) + dot(vs_grad[...], weights[0])).astype(BF16)
     query_part, key_part = attend_scores_back(chance_t, tq, tk, value_t, at_grad)
-    tq_grad[...] = query_part.astype(BF16)
-    tk_grad[...] = key_part.astype(BF16)
+    rows_one[...] = query_part
+    rows_two[...] = key_part
+    split_pairs(rows_one, tq_grad)
+    split_pairs(rows_two, tk_grad)
 
     first_end(0, first_s)
     second_s = second_ring(0)
@@ -456,6 +474,15 @@
         copy.wait_send()
 
 
+def hand_over(*refs):
+    semaphores = refs[12]
+    copies = [pltpu.make_async_copy(refs[at], refs[6 + at], semaphores.at[at]) for at in range(6)]
+    for copy in copies:
+        copy.start()
+    for copy in copies:
+        copy.wait()
+
+
 def body(
     block_input, spatial_queries, spatial_keys, cotangent, temporal_queries, temporal_keys, weights
 ):
@@ -463,17 +490,19 @@
     tables = make_tables()
     arrays = [
         block_input.reshape(TOKENS, WIDTH),
-        spatial_queries.reshape(TOKENS, INNER),
-        spatial_keys.reshape(TOKENS, INNER),
-        cotangent.reshape(TOKENS, WIDTH),
-        temporal_queries.reshape(TOKENS, INNER),
-        temporal_keys.reshape(TOKENS, INNER),
-        weights,
+        spatial_queries.reshape(TOKENS, INNER).T,
+        spatial_keys.reshape(TOKENS, INNER).T,
+        cotangent.reshape(FRAMES, 2, WIDTH),
+        temporal_queries.reshape(FRAMES, 2, INNER),
+        temporal_keys.reshape(FRAMES, 2, INNER),
+        weights.transpose(0, 2, 1),
     ] + tables
     wide, narrow = (TOKENS, WIDTH), (TOKENS, INNER)
     chances = pltpu.VMEM((HEADS, TOKENS, TOKENS), F32)
     dma = pltpu.SemaphoreType.DMA
     scratch = [pltpu.VMEM(array.shape, BF16) for array in arrays]
+    scratch += [pltpu.VMEM(narrow, BF16)] * 2 + [pltpu.VMEM(wide, BF16)] + [pltpu.VMEM(narrow, BF16)] * 2
+    scratch += [pltpu.VMEM(wide, F32)] + [pltpu.VMEM(narrow, F32)] * 2
     scratch += [chances, chances] + [pltpu.VMEM(narrow, BF16)] * 8
     scratch += [pltpu.VMEM(wide, BF16)] * 2 + [pltpu.VMEM((2,) + wide, BF16)] * 4
     scratch += [
@@ -488,10 +517,17 @@
         pltpu.VMEM((2, 7, SHARE_ROWS, LANES), BF16),
     ]
     scratch += [dma((14,))] + [dma((2, 7))] * 4 + [dma((4,))] * 4 + [dma((2, 6))] * 4 + [dma((2, 7))] * 2
-    bf16_out = [jax.ShapeDtypeStruct(wide, BF16)] + [jax.ShapeDtypeStruct(narrow, BF16)] * 4
-    input_grad, sq_grad, sk_grad, tq_grad, tk_grad, weight_grads = pl.pallas_call(
+    results = [
+        jax.ShapeDtypeStruct(wide, BF16),
+        jax.ShapeDtypeStruct((INNER, TOKENS), BF16),
+        jax.ShapeDtypeStruct((INNER, TOKENS), BF16),
+        jax.ShapeDtypeStruct((FRAMES, 2, INNER), BF16),
+        jax.ShapeDtypeStruct((FRAMES, 2, INNER), BF16),
+        jax.ShapeDtypeStruct((18, 4, 144), F32),
+    ]
+    made = pl.pallas_call(
         functools.partial(kernel, grad_scale),
-        out_shape=bf16_out + [jax.ShapeDtypeStruct((4, 18, 144), F32)],
+        out_shape=results,
         in_specs=[pl.BlockSpec(memory_space=pl.ANY)] * len(arrays),
         out_specs=[pl.BlockSpec(memory_space=pltpu.VMEM)] * 6,
         scratch_shapes=scratch,
@@ -500,13 +536,22 @@
         ),
         name="block_backward",
     )(*arrays)
+    input_grad, sq_grad, sk_grad, tq_grad, tk_grad, weight_grads = pl.pallas_call(
+        hand_over,
+        out_shape=results,
+        in_specs=[pl.BlockSpec(memory_space=pl.ANY)] * 6,
+        out_specs=[pl.BlockSpec(memory_space=pl.ANY)] * 6,
+        scratch_shapes=[pltpu.SemaphoreType.DMA((6,))],
+        compiler_params=pltpu.CompilerParams(vmem_limit_bytes=60 * 2**20),
+        name="hand_over",
+    )(*made)
     return (
         input_grad.reshape(block_input.shape),
-        sq_grad.reshape(spatial_queries.shape),
-        sk_grad.reshape(spatial_keys.shape),
+        sq_grad.T.reshape(spatial_queries.shape),
+        sk_grad.T.reshape(spatial_keys.shape),
         tq_grad.reshape(temporal_queries.shape),
         tk_grad.reshape(temporal_keys.shape),
-        weight_grads,
+        weight_grads.transpose(1, 0, 2),
     )
 
 

time: 96.3 us -> 100 us (1.038)
  Pallas kernels: 67.6 us -> 98.8 us
  local copies, waits for them, and re-layouts: 27.1 us -> 0 us
    pallas_call x1 -> x2, Pallas kernels: 67.6 us -> 98.8 us  [the longest x1 67.6 us: body(): pl.pallas_call(functools.partial(kernel, grad_scale), out_shape=results,...]
    unnamed x7 -> x0, local copies, waits for them, and re-layouts: 18.6 us -> none
    reshape x5 -> x0, local copies, waits for them, and re-layouts: 8.51 us -> none  [the longest x1 1.78 us: body(): cotangent.reshape(TOKENS, WIDTH)]
where the time goes in v3:
time: 100 us; the launch traced here: 99.6 us
  Pallas kernels  98.8 us (99%)
    pallas_call x1, Pallas kernels, body(): pl.pallas_call(functools.partial(kernel, grad_scale), out_shape=results,...  67.6 us
    pallas_call x1, Pallas kernels, body(): pl.pallas_call(hand_over, out_shape=results, in_specs=[pl.BlockSpec(memor...  31.2 us

profile of v3, /device:TPU:4, one launch (start us, length us, event | category | flops | bytes accessed | tf_op | source)
XLA Modules:
  0.0 99.6 jit_solution(7335681345980698643)
XLA Ops:
  0.6 67.6 %block_backward.1 = (bf16[128,1152]{1,0:T(8,128)(2,1)}, bf16[576,128]{1,0:T(8,128)(2,1)}, bf16[576,128]{1,0:T(8,128)(2,1)}, bf16[64,2,576]{2,1,0:T(2,128)(2,1)},...) custom-call(bf16[128,1152]{1,0:T(8,128)(2,1)} %bitcast.22, bf16[576,128]{1,0:T(8,128)(2,1)} %bitcast.26, ...), custom_call_target="tpu_custom_call" | custom-call | tf_op jit(solution)/shard_map/block_backward/pallas_call | solution.py:528
  68.3 31.2 %hand_over.1 = (bf16[128,1152]{1,0:T(8,128)(2,1)}, bf16[576,128]{1,0:T(8,128)(2,1)}, bf16[576,128]{1,0:T(8,128)(2,1)}, bf16[64,2,576]{2,1,0:T(2,128)(2,1)}, bf16...) custom-call(bf16[128,1152]{1,0:T(8,128)(2,1)} %get-tuple-element.18.refs_0_, bf16[576,128]{1,0:T(8,128)(2,1)} %get-tuple-element.19.refs_1_, ...), custom_call_target="tpu_custom_call" | custom-call | tf_op jit(solution)/shard_map/hand_over/pallas_call | solution.py:539

commit v4 on v3

--- a/solution.py
+++ b/solution.py
@@ -41,7 +41,8 @@
     to_natural = [
         (y * 4 + x) * 16 + z * 2 + p for y in range(2) for z in range(8) for x in range(4) for p in range(2)
     ]
-    token_moves = np.stack([one_hot(order, TOKENS) for order in (to_z, to_plane, to_natural)])
+    forth = [one_hot(order, TOKENS) for order in (to_z, to_plane, to_natural)]
+    token_moves = np.stack(forth + [table.T for table in forth])
     feature_moves = np.stack(
         [
             one_hot(
@@ -60,6 +61,12 @@
     return [jnp.asarray(table, BF16) for table in (token_moves, feature_moves, picks, share_moves)]
 
 
+def line_order(frame):
+    y_lo, z, x = frame // 32, frame // 4 % 8, frame % 4
+    start = 2 * (z * 8 + y_lo * 4 + x)
+    return slice(start, start + 2)
+
+
 def dot(left, right):
     return jnp.dot(left, right, preferred_element_type=F32)
 
@@ -141,8 +148,8 @@
     block, sq_turned, sk_turned, cot_pairs, tq_pairs, tk_pairs, weights, token_moves, feature_moves, picks, share_moves,
     sq, sk, cot, tq, tk, rows_wide, rows_one, rows_two,
     chance_s, chance_t, value_s, value_t, attended_s, attended_t, at_grad, as_grad, vt_grad, vs_grad,
-    mixed, mixed_grad,
-    out_z, in_z, out_plane, in_plane,
+    mixed, mixed_grad, cot_frame, vt_grad_frame,
+    in_z_wide, out_plane_wide, in_plane_wide, out_plane, in_plane, out_z, in_z,
     factors, picked, picked_out, sums, arrived, sums_two, arrived_two, shares, shares_in,
     load_sem, z_send, z_recv, plane_send, plane_recv, factor_send, factor_recv, picked_send, picked_recv,
     ring_send, ring_recv, ring_two_send, ring_two_recv, share_send, share_recv,
@@ -175,9 +182,9 @@
     loads = []
     for number, (source, target) in enumerate(
         [
-            (tq_hbm, tq_pairs), (tk_hbm, tk_pairs), (cot_hbm, cot_pairs), (weights_hbm.at[3], weights.at[3]),
-            (weights_hbm.at[2], weights.at[2]), (token_moves_hbm, token_moves), (block_hbm, block),
-            (weights_hbm.at[0], weights.at[0]), (sq_hbm, sq_turned), (sk_hbm, sk_turned), (weights_hbm.at[1], weights.at[1]),
+            (cot_hbm, cot_pairs), (tq_hbm, tq_pairs), (tk_hbm, tk_pairs), (weights_hbm.at[3], weights.at[3]),
+            (token_moves_hbm, token_moves), (block_hbm, block), (weights_hbm.at[0], weights.at[0]),
+            (sq_hbm, sq_turned), (sk_hbm, sk_turned), (weights_hbm.at[1], weights.at[1]), (weights_hbm.at[2], weights.at[2]),
             (feature_moves_hbm, feature_moves), (picks_hbm, picks), (share_moves_hbm, share_moves),
         ]
     ):
@@ -205,32 +212,32 @@
     def move_tokens(number, rows):
         return dot(token_moves[number], rows).astype(BF16)
 
-    def start_z(item):
+    def start_z(item, source, target):
         copies = []
         for step in range(1, 8):
             to = (z + step) % 8
             copies.append(
                 send(
-                    out_z.at[item, pl.ds(to * 16, 16)], in_z.at[item, pl.ds(z * 16, 16)],
+                    source.at[pl.ds(to * 16, 16)], target.at[pl.ds(z * 16, 16)],
                     z_send.at[item, step - 1], z_recv.at[item, step - 1], along_z(step),
                 )
             )
         own = pl.ds(pl.multiple_of(z * 16, 16), 16)
-        in_z[item, own, :] = out_z[item, own, :]
+        target[own, :] = source[own, :]
         return copies
 
-    def start_plane(item):
+    def start_plane(item, source, target):
         copies = []
         for step in range(1, 8):
             to = (q + step) % 8
             copies.append(
                 send(
-                    out_plane.at[item, pl.ds(to * 16, 16)], in_plane.at[item, pl.ds(q * 16, 16)],
+                    source.at[pl.ds(to * 16, 16)], target.at[pl.ds(q * 16, 16)],
                     plane_send.at[item, step - 1], plane_recv.at[item, step - 1], in_the_plane(step),
                 )
             )
         own = pl.ds(pl.multiple_of(q * 16, 16), 16)
-        in_plane[item, own, :] = out_plane[item, own, :]
+        target[own, :] = source[own, :]
         return copies
 
     def arrive(copies):
@@ -381,71 +388,76 @@
 
     def join_pairs(pairs, rows):
         for frame in range(FRAMES):
-            rows[2 * frame : 2 * frame + 2, :] = pairs[frame].astype(F32)
+            rows[line_order(frame), :] = pairs[frame].astype(F32)
         return rows[...].astype(BF16)
 
     def split_pairs(rows, pairs):
         for frame in range(FRAMES):
-            pairs[frame] = rows[2 * frame : 2 * frame + 2, :].astype(BF16)
+            pairs[frame] = rows[line_order(frame), :].astype(BF16)
 
     loads[0].wait()
+    cot[...] = join_pairs(cot_pairs, rows_wide)
+    pl.semaphore_wait(barrier, len(greeted))
+    cot_z = start_z(0, cot, in_z_wide)
     loads[1].wait()
+    loads[2].wait()
     tq[...] = join_pairs(tq_pairs, rows_one)
     tk[...] = join_pairs(tk_pairs, rows_two)
     row_patch = lax.broadcasted_iota(jnp.int32, (TOKENS, TOKENS), 0) % 2
     column_patch = lax.broadcasted_iota(jnp.int32, (TOKENS, TOKENS), 1) % 2
     softmax_heads(tq, tk, chance_t, jnp.where(row_patch == column_patch, 0.0, -1e30))
-    loads[2].wait()
     loads[3].wait()
-    cot[...] = join_pairs(cot_pairs, rows_wide)
+    loads[4].wait()
     at_grad[...] = dot_nt(cot[...], weights[3]).astype(BF16)
     vt_grad[...] = attend_values_back(chance_t, at_grad).astype(BF16)
-    loads[4].wait()
-    loads[5].wait()
-    out_z[1] = move_tokens(0, (cot[...].astype(F32) + dot(vt_grad[...], weights[2])).astype(BF16))
-    pl.semaphore_wait(barrier, len(greeted))
-    grad_z = start_z(1)
-
-    for number in (6, 7, 8, 9, 10):
+    out_plane[0] = move_tokens(1, vt_grad[...])
+    grad_plane = start_plane(1, out_plane.at[0], in_plane.at[0])
+
+    for number in (5, 6, 7, 8, 9, 10):
         loads[number].wait()
     sq[...] = sq_turned[...].T
     sk[...] = sk_turned[...].T
     value_s[...] = dot_nt(block[...], weights[0]).astype(BF16)
     softmax_heads(sq, sk, chance_s, None)
     attended_s[...] = attend(chance_s, value_s).astype(BF16)
-    out_z[0] = move_tokens(0, (block[...].astype(F32) + dot(attended_s[...], weights[1])).astype(BF16))
-    mixed_z = start_z(0)
-
+    mixed[...] = (block[...].astype(F32) + dot(attended_s[...], weights[1])).astype(BF16)
+    out_plane[1] = move_tokens(5, dot_nt(mixed[...], weights[2]).astype(BF16))
+    value_plane = start_plane(2, out_plane.at[1], in_plane.at[1])
+
+    arrive(grad_plane)
+    out_z[0] = move_tokens(4, in_plane[0])
+    grad_z = start_z(1, out_z.at[0], in_z.at[0])
     for number in (11, 12, 13):
         loads[number].wait()
-    arrive(grad_z)
-    out_plane[1] = move_tokens(1, in_z[1])
-    grad_plane = start_plane(1)
     feature_copies, column_copies = {}, {}
     feature_copies[0] = start_features(0, block)
+    column_copies[1] = start_columns(1, attended_s[...])
+    arrive(cot_z)
+    out_plane_wide[...] = move_tokens(1, in_z_wide[...])
+    cot_plane = start_plane(0, out_plane_wide, in_plane_wide)
+    arrive(value_plane)
+    out_z[1] = move_tokens(4, in_plane[1])
+    value_z = start_z(2, out_z.at[1], in_z.at[1])
+    feature_copies[2] = start_features(2, mixed)
     feature_copies[3] = start_features(3, cot)
-    column_copies[1] = start_columns(1, attended_s[...])
-    column_copies[2] = start_columns(2, vt_grad[...])
-    arrive(mixed_z)
-    out_plane[0] = move_tokens(1, in_z[0])
-    mixed_plane = start_plane(0)
-
-    arrive(grad_plane)
-    mixed_grad[...] = move_tokens(2, in_plane[1])
+
+    arrive(cot_plane)
+    cot_frame[...] = move_tokens(2, in_plane_wide[...])
+    arrive(grad_z)
+    vt_grad_frame[...] = move_tokens(3, in_z[0])
+    mixed_grad[...] = (cot_frame[...].astype(F32) + dot(vt_grad_frame[...], weights[2])).astype(BF16)
     feature_copies[1] = start_features(1, mixed_grad)
     as_grad[...] = dot_nt(mixed_grad[...], weights[1]).astype(BF16)
     vs_grad[...] = attend_values_back(chance_s, as_grad).astype(BF16)
     column_copies[0] = start_columns(0, vs_grad[...])
-
-    arrive(mixed_plane)
-    mixed[...] = move_tokens(2, in_plane[0])
-    feature_copies[2] = start_features(2, mixed)
-    value_t[...] = dot_nt(mixed[...], weights[2]).astype(BF16)
+    column_copies[2] = start_columns(2, vt_grad_frame[...])
+
+    arrive([feature_copies[0], feature_copies[1], column_copies[0], column_copies[1]])
+    first_s = first_ring(0)
+    arrive(value_z)
+    value_t[...] = in_z[1]
     attended_t[...] = attend(chance_t, value_t).astype(BF16)
     column_copies[3] = start_columns(3, attended_t[...])
-
-    arrive([feature_copies[0], feature_copies[1], column_copies[0], column_copies[1]])
-    first_s = first_ring(0)
     arrive([feature_copies[2], feature_copies[3], column_copies[2], column_copies[3]])
     first_t = first_ring(1)
     first_relay(0, first_s)
@@ -475,12 +487,8 @@
 
 
 def hand_over(*refs):
-    semaphores = refs[12]
-    copies = [pltpu.make_async_copy(refs[at], refs[6 + at], semaphores.at[at]) for at in range(6)]
-    for copy in copies:
-        copy.start()
-    for copy in copies:
-        copy.wait()
+    for at in range(6):
+        refs[6 + at][...] = refs[at][...]
 
 
 def body(
@@ -504,7 +512,8 @@
     scratch += [pltpu.VMEM(narrow, BF16)] * 2 + [pltpu.VMEM(wide, BF16)] + [pltpu.VMEM(narrow, BF16)] * 2
     scratch += [pltpu.VMEM(wide, F32)] + [pltpu.VMEM(narrow, F32)] * 2
     scratch += [chances, chances] + [pltpu.VMEM(narrow, BF16)] * 8
-    scratch += [pltpu.VMEM(wide, BF16)] * 2 + [pltpu.VMEM((2,) + wide, BF16)] * 4
+    scratch += [pltpu.VMEM(wide, BF16)] * 3 + [pltpu.VMEM(narrow, BF16)]
+    scratch += [pltpu.VMEM(wide, BF16)] * 3 + [pltpu.VMEM((2,) + narrow, BF16)] * 4
     scratch += [
         pltpu.VMEM((4, WIDTH, 2 * TOKENS), BF16),
         pltpu.VMEM((4, 2, 2 * TOKENS, LANES), BF16),
@@ -516,7 +525,7 @@
         pltpu.VMEM((2, 8 * SHARE_ROWS, LANES), BF16),
         pltpu.VMEM((2, 7, SHARE_ROWS, LANES), BF16),
     ]
-    scratch += [dma((14,))] + [dma((2, 7))] * 4 + [dma((4,))] * 4 + [dma((2, 6))] * 4 + [dma((2, 7))] * 2
+    scratch += [dma((14,))] + [dma((3, 7))] * 4 + [dma((4,))] * 4 + [dma((2, 6))] * 4 + [dma((2, 7))] * 2
     results = [
         jax.ShapeDtypeStruct(wide, BF16),
         jax.ShapeDtypeStruct((INNER, TOKENS), BF16),
@@ -539,9 +548,8 @@
     input_grad, sq_grad, sk_grad, tq_grad, tk_grad, weight_grads = pl.pallas_call(
         hand_over,
         out_shape=results,
-        in_specs=[pl.BlockSpec(memory_space=pl.ANY)] * 6,
-        out_specs=[pl.BlockSpec(memory_space=pl.ANY)] * 6,
-        scratch_shapes=[pltpu.SemaphoreType.DMA((6,))],
+        in_specs=[pl.BlockSpec(memory_space=pltpu.VMEM)] * 6,
+        out_specs=[pl.BlockSpec(memory_space=pltpu.VMEM)] * 6,
         compiler_params=pltpu.CompilerParams(vmem_limit_bytes=60 * 2**20),
         name="hand_over",
     )(*made)

time: 100 us -> 70.1 us (0.70)
  Pallas kernels: 98.8 us -> 69.4 us
    pallas_call x1, Pallas kernels: 31.2 us -> 2.2 us  [body(): pl.pallas_call(hand_over, out_shape=results, in_specs=[pl.BlockSpec(memor...]
where the time goes in v4:
time: 70.1 us; the launch traced here: 70 us
  Pallas kernels  69.4 us (99%)
    pallas_call x1, Pallas kernels, body(): pl.pallas_call(functools.partial(kernel, grad_scale), out_shape=results,...  67.2 us
    pallas_call x1, Pallas kernels, body(): pl.pallas_call(hand_over, out_shape=results, in_specs=[pl.BlockSpec(memor...  2.2 us

profile of v4, /device:TPU:4, one launch (start us, length us, event | category | flops | bytes accessed | tf_op | source)
XLA Modules:
  0.0 70.0 jit_solution(2793426655287862587)
XLA Ops:
  0.6 67.2 %block_backward.1 = (bf16[128,1152]{1,0:T(8,128)(2,1)}, bf16[576,128]{1,0:T(8,128)(2,1)}, bf16[576,128]{1,0:T(8,128)(2,1)}, bf16[64,2,576]{2,1,0:T(2,128)(2,1)},...) custom-call(bf16[128,1152]{1,0:T(8,128)(2,1)} %bitcast.22, bf16[576,128]{1,0:T(8,128)(2,1)} %bitcast.26, ...), custom_call_target="tpu_custom_call" | custom-call | tf_op jit(solution)/shard_map/block_backward/pallas_call | solution.py:537
  67.8 2.2 %hand_over.1 = (bf16[128,1152]{1,0:T(8,128)(2,1)}, bf16[576,128]{1,0:T(8,128)(2,1)}, bf16[576,128]{1,0:T(8,128)(2,1)}, bf16[64,2,576]{2,1,0:T(2,128)(2,1)}, bf16...) custom-call(bf16[128,1152]{1,0:T(8,128)(2,1)} %get-tuple-element.18.refs_0_, bf16[576,128]{1,0:T(8,128)(2,1)} %get-tuple-element.19.refs_1_, ...), custom_call_target="tpu_custom_call" | custom-call | tf_op jit(solution)/shard_map/hand_over/pallas_call | solution.py:548

commit v5 on v4

--- a/solution.py
+++ b/solution.py
@@ -17,8 +17,11 @@
 SCORE_SCALE = HEAD_DIM ** (-0.5)
 ROW_BLOCK = 144
 LANES = 384
-SHARE_ROWS = 32
-CUT = 80
+PIECE = 9 * ROW_BLOCK
+CUT = 640
+BLOCK_ROWS = 2 * ROW_BLOCK + 48
+SHARE_ROWS = 96
+PAIRS = ((1, 2), (0, 3))
 F32 = jnp.float32
 BF16 = jnp.bfloat16
 MESH = pl.DeviceIdType.MESH
@@ -57,8 +60,25 @@
             for y_hi in range(2):
                 for column in range(144):
                     picks[core, matrix, y_hi, (2 * y_hi + core) * 144 + column, matrix * 144 + column] = 1.0
-    share_moves = one_hot([z * 18 + r if r < 18 else -1 for z in range(8) for r in range(SHARE_ROWS)], ROW_BLOCK)
-    return [jnp.asarray(table, BF16) for table in (token_moves, feature_moves, picks, share_moves)]
+    share_moves = one_hot(
+        [
+            part * 144 + z * 18 + r if part < 4 else -1
+            for z in range(8)
+            for part, r in [divmod(row, 18) for row in range(80)]
+        ],
+        4 * ROW_BLOCK,
+    )
+    rest_moves = []
+    for group in range(4):
+        source = []
+        for z in range(8):
+            for row in range(16):
+                at = z * 18 + 9 * (group % 2) + row
+                place, turn = at // 16, (group - at // 16) % 4
+                source.append(turn * 48 + place // 4 * 16 + at % 16 if row < 9 else -1)
+        rest_moves.append(one_hot(source, 192))
+    tables = (token_moves, feature_moves, picks, share_moves, np.stack(rest_moves))
+    return [jnp.asarray(table, BF16) for table in tables]
 
 
 def line_order(frame):
@@ -143,14 +163,14 @@
 def kernel(
     grad_scale,
     block_hbm, sq_hbm, sk_hbm, cot_hbm, tq_hbm, tk_hbm, weights_hbm,
-    token_moves_hbm, feature_moves_hbm, picks_hbm, share_moves_hbm,
+    token_moves_hbm, feature_moves_hbm, picks_hbm, share_moves_hbm, rest_moves_hbm,
     input_grad, sq_grad, sk_grad, tq_grad, tk_grad, weight_grads,
-    block, sq_turned, sk_turned, cot_pairs, tq_pairs, tk_pairs, weights, token_moves, feature_moves, picks, share_moves,
+    block, sq_turned, sk_turned, cot_pairs, tq_pairs, tk_pairs, weights, token_moves, feature_moves, picks, share_moves, rest_moves,
     sq, sk, cot, tq, tk, rows_wide, rows_one, rows_two,
     chance_s, chance_t, value_s, value_t, attended_s, attended_t, at_grad, as_grad, vt_grad, vs_grad,
     mixed, mixed_grad, cot_frame, vt_grad_frame,
     in_z_wide, out_plane_wide, in_plane_wide, out_plane, in_plane, out_z, in_z,
-    factors, picked, picked_out, sums, arrived, sums_two, arrived_two, shares, shares_in,
+    factors, picked, picked_out, sums, arrived, total_one, sums_two, arrived_two, shares, shares_in, total_share,
     load_sem, z_send, z_recv, plane_send, plane_recv, factor_send, factor_recv, picked_send, picked_recv,
     ring_send, ring_recv, ring_two_send, ring_two_recv, share_send, share_recv,
 ):
@@ -186,10 +206,12 @@
             (token_moves_hbm, token_moves), (block_hbm, block), (weights_hbm.at[0], weights.at[0]),
             (sq_hbm, sq_turned), (sk_hbm, sk_turned), (weights_hbm.at[1], weights.at[1]), (weights_hbm.at[2], weights.at[2]),
             (feature_moves_hbm, feature_moves), (picks_hbm, picks), (share_moves_hbm, share_moves),
+            (rest_moves_hbm, rest_moves),
         ]
     ):
         copy = pltpu.make_async_copy(source, target, load_sem.at[number])
-        copy.start()
+        if number < 11:
+            copy.start()
         loads.append(copy)
 
     barrier = pltpu.get_barrier_semaphore()
@@ -256,39 +278,42 @@
 
     def start_columns(number, rows):
         for side in range(2):
-            picked[number, side, 0:TOKENS, :] = dot(rows, picks[core, number % 2, side]).astype(BF16)
-            picked_out[number, side] = dot(rows, picks[1 - core, number % 2, side]).astype(BF16)
+            place = 0 if number < 2 else 1
+            picked[number, side, 0:TOKENS, :] = dot(rows, picks[core, place, side]).astype(BF16)
+            picked_out[number, side] = dot(rows, picks[1 - core, place, side]).astype(BF16)
         return send(
             picked_out.at[number], picked.at[number, :, TOKENS : 2 * TOKENS],
             picked_send.at[number], picked_recv.at[number], sibling,
         )
 
-    def block_sum(pair, side, y_lo_at, x_at):
-        rows = pl.ds(pl.multiple_of((y_lo_at * 4 + x_at) * ROW_BLOCK, 16), ROW_BLOCK)
-        total = dot(factors[2 * pair, rows, :], picked[2 * pair, side])
-        total += dot(factors[2 * pair + 1, rows, :], picked[2 * pair + 1, side])
-        sums[pair, side, y_lo_at, x_at] = total.astype(BF16)
+    def make_pieces(pair, to):
+        rests = None
+        for sub in range(4):
+            side, y_lo_at, x_at = (sub // 2, sub % 2, to) if pair == 0 else (to // 2, to % 2, sub)
+            rows = pl.ds(pl.multiple_of((y_lo_at * 4 + x_at) * ROW_BLOCK, 16), ROW_BLOCK)
+            one, two = PAIRS[pair]
+            total = dot(factors[one, rows, :], picked[one, side]) + dot(factors[two, rows, :], picked[two, side])
+            at = 2 * sub * ROW_BLOCK
+            sums[pair, to, at : at + ROW_BLOCK, :] = total[:, 0:128].astype(BF16)
+            sums[pair, to, at + ROW_BLOCK : at + 2 * ROW_BLOCK, :] = total[:, 128:256].astype(BF16)
+            rest = total[:, 256:384]
+            rests = rest if sub == 0 else rests + pltpu.roll(rest, 32 * sub, 1)
+        sums[pair, to, 8 * ROW_BLOCK : PIECE, :] = rests.astype(BF16)
 
     def piece(pair, to, half):
-        if pair == 0:
-            return sums.at[0, half, :, to]
-        return sums.at[1, to // 2, to % 2, 2 * half : 2 * half + 2]
-
-    def make_pieces(pair, to):
-        if pair == 0:
-            for side in range(2):
-                for y_lo_at in range(2):
-                    block_sum(0, side, y_lo_at, to)
-        else:
-            for x_at in range(4):
-                block_sum(1, to // 2, to % 2, x_at)
+        return sums.at[pair, to, 0:CUT] if half == 0 else sums.at[pair, to, CUT:PIECE]
+
+    slot_half = (0, 1, 1, 0, 0, 1)
+
+    def slot_ref(pair, slot):
+        return arrived.at[pair, slot, 0 : (CUT if slot_half[slot] == 0 else PIECE - CUT)]
 
     places = (x, y)
     rings = (along_x, along_y)
 
     def ring_copy(pair, slot, source):
         peer = rings[pair](1 if slot % 2 == 0 else -1 + 4)
-        return send(source, arrived.at[pair, slot], ring_send.at[pair, slot], ring_recv.at[pair, slot], peer)
+        return send(source, slot_ref(pair, slot), ring_send.at[pair, slot], ring_recv.at[pair, slot], peer)
 
     def first_ring(pair):
         place = places[pair]
@@ -310,81 +335,89 @@
         for slot, to, half in ((0, after, 0), (1, before, 1)):
             copies[slot].wait_recv()
             ref = piece(pair, to, half)
-            ref[...] = (ref[...].astype(F32) + arrived[pair, slot].astype(F32)).astype(BF16)
+            ref[...] = (ref[...].astype(F32) + slot_ref(pair, slot)[...].astype(F32)).astype(BF16)
             copies[slot + 4] = ring_copy(pair, slot + 4, ref)
+
+    lane_group = lax.broadcasted_iota(jnp.int32, (16, 128), 1) // 32
 
     def first_end(pair, copies):
         for half, slots in ((0, (3, 4)), (1, (2, 5))):
             total = piece(pair, places[pair], half)[...].astype(F32)
             for slot in slots:
                 copies[slot].wait_recv()
-                total += arrived[pair, slot].astype(F32)
-            sums_two[pair, 2 * half : 2 * half + 2] = total.astype(BF16)
-
-    def part_two(pair, to, half):
-        return sums_two.at[pair, to, 0:CUT] if half == 0 else sums_two.at[pair, to, CUT:ROW_BLOCK]
-
-    def slot_two(pair, slot, half):
-        return arrived_two.at[pair, slot, 0 : (CUT if half == 0 else ROW_BLOCK - CUT)]
-
-    slot_half = (0, 1, 1, 0, 0, 1)
-
-    def ring_two_copy(pair, slot, source):
-        peer = rings[1 - pair](1 if slot % 2 == 0 else -1 + 4)
-        return send(
-            source, slot_two(pair, slot, slot_half[slot]),
-            ring_two_send.at[pair, slot], ring_two_recv.at[pair, slot], peer,
-        )
+                total += slot_ref(pair, slot)[...].astype(F32)
+            total_one[(0 if half == 0 else CUT) : (CUT if half == 0 else PIECE), :] = total
+        for sub in range(4):
+            at = 2 * sub * ROW_BLOCK
+            sums_two[pair, sub, 0 : 2 * ROW_BLOCK, :] = total_one[at : at + 2 * ROW_BLOCK, :].astype(BF16)
+            for tile in range(3):
+                packed = jnp.zeros((16, 128), F32)
+                for group in range(4 if tile < 2 else 1):
+                    start = 8 * ROW_BLOCK + 16 * (4 * tile + group)
+                    rest = pltpu.roll(total_one[start : start + 16, :], 32 * ((group - sub) % 4), 1)
+                    packed = jnp.where(lane_group == group, rest, packed)
+                start = 2 * ROW_BLOCK + 16 * tile
+                sums_two[pair, sub, start : start + 16, :] = packed.astype(BF16)
 
     def second_ring(pair):
         place = places[1 - pair]
-        after, across, before = (place + 1) % 4, (place + 2) % 4, (place + 3) % 4
-        copies = {}
-        copies[0] = ring_two_copy(pair, 0, part_two(pair, across, 0))
-        copies[1] = ring_two_copy(pair, 1, part_two(pair, across, 1))
-        copies[2] = ring_two_copy(pair, 2, part_two(pair, after, 1))
-        copies[3] = ring_two_copy(pair, 3, part_two(pair, before, 0))
-        return copies
-
-    def second_relay(pair, copies):
-        place = places[1 - pair]
-        after, before = (place + 1) % 4, (place + 3) % 4
-        for slot, to, half in ((0, after, 0), (1, before, 1)):
-            copies[slot].wait_recv()
-            ref = part_two(pair, to, half)
-            ref[...] = (ref[...].astype(F32) + slot_two(pair, slot, half)[...].astype(F32)).astype(BF16)
-            copies[slot + 4] = ring_two_copy(pair, slot + 4, ref)
-
-    def second_end(pair, copies):
-        place = places[1 - pair]
-        halves = []
-        for half, slots in ((0, (3, 4)), (1, (2, 5))):
-            total = part_two(pair, place, half)[...].astype(F32)
-            for slot in slots:
-                copies[slot].wait_recv()
-                total += slot_two(pair, slot, half)[...].astype(F32)
-            halves.append(total.astype(BF16))
-        shares[pair] = dot(share_moves[...], jnp.concatenate(halves, axis=0)).astype(BF16)
-        last = []
-        for step in range(1, 8):
-            to = (z + step) % 8
-            last.append(
+        copies = []
+        for step in range(1, 4):
+            copies.append(
                 send(
-                    shares.at[pair, pl.ds(to * SHARE_ROWS, SHARE_ROWS)], shares_in.at[pair, step - 1],
-                    share_send.at[pair, step - 1], share_recv.at[pair, step - 1], along_z(step),
+                    sums_two.at[pair, (place + step) % 4], arrived_two.at[pair, step - 1],
+                    ring_two_send.at[pair, step - 1], ring_two_recv.at[pair, step - 1], rings[1 - pair](step),
                 )
             )
-        return last
-
-    def finish(pair, copies):
-        own = pl.ds(pl.multiple_of(z * SHARE_ROWS, SHARE_ROWS), SHARE_ROWS)
-        total = shares[pair, own, :].astype(F32)
+        return copies
+
+    def second_end(pair, copies):
+        total = sums_two[pair, places[1 - pair]].astype(F32)
+        for step in range(1, 4):
+            copies[step - 1].wait_recv()
+            total += arrived_two[pair, step - 1].astype(F32)
+        return total
+
+    def last_line(totals):
+        whole = jnp.concatenate([total[0 : 2 * ROW_BLOCK] for total in totals], axis=0).astype(BF16)
+        moved = dot(share_moves[...], whole).astype(BF16)
+        rest = jnp.zeros((TOKENS, 128), F32)
+        lanes = lax.broadcasted_iota(jnp.int32, (TOKENS, 128), 1) // 32
+        for pair, total in enumerate(totals):
+            ends = total[2 * ROW_BLOCK : BLOCK_ROWS]
+            turned = [ends] + [pltpu.roll(ends, 32 * turn, 1) for turn in range(1, 4)]
+            turned = jnp.concatenate(turned, axis=0).astype(BF16)
+            for group in (2 * pair, 2 * pair + 1):
+                rest = jnp.where(lanes == group, dot(rest_moves[group], turned), rest)
+        rest = rest.astype(BF16)
+        for z_at in range(8):
+            shares[z_at, 0:80, :] = moved[80 * z_at : 80 * z_at + 80]
+            shares[z_at, 80:96, :] = rest[16 * z_at : 16 * z_at + 16]
+        copies = []
+        for step in range(1, 8):
+            copies.append(
+                send(
+                    shares.at[(z + step) % 8], shares_in.at[step - 1],
+                    share_send.at[step - 1], share_recv.at[step - 1], along_z(step),
+                )
+            )
+        return copies
+
+    def finish(copies):
+        total = shares[z].astype(F32)
         for step in range(1, 8):
             copies[step - 1].wait_recv()
-            total += shares_in[pair, step - 1].astype(F32)
-        total = total * grad_scale
-        weight_grads[:, 2 * pair, :] = total[0:18, 0:144]
-        weight_grads[:, 2 * pair + 1, :] = total[0:18, 144:288]
+            total += shares_in[step - 1].astype(F32)
+        total_share[...] = total * grad_scale
+        for pair, (one, two) in enumerate(PAIRS):
+            left = total_share[36 * pair : 36 * pair + 18, :]
+            right = total_share[36 * pair + 18 : 36 * pair + 36, :]
+            weight_grads[:, one, 0:128] = left
+            weight_grads[:, one, 128:144] = right[:, 0:16]
+            weight_grads[:, two, 0:112] = right[:, 16:128]
+            for half in range(2):
+                start = 64 * pair + 32 * half
+                weight_grads[9 * half : 9 * half + 9, two, 112:144] = total_share[80:89, start : start + 32]
 
     def join_pairs(pairs, rows):
         for frame in range(FRAMES):
@@ -399,6 +432,8 @@
     cot[...] = join_pairs(cot_pairs, rows_wide)
     pl.semaphore_wait(barrier, len(greeted))
     cot_z = start_z(0, cot, in_z_wide)
+    for copy in loads[11:]:
+        copy.start()
     loads[1].wait()
     loads[2].wait()
     tq[...] = join_pairs(tq_pairs, rows_one)
@@ -427,7 +462,7 @@
     arrive(grad_plane)
     out_z[0] = move_tokens(4, in_plane[0])
     grad_z = start_z(1, out_z.at[0], in_z.at[0])
-    for number in (11, 12, 13):
+    for number in (11, 12, 13, 14):
         loads[number].wait()
     feature_copies, column_copies = {}, {}
     feature_copies[0] = start_features(0, block)
@@ -445,26 +480,26 @@
     cot_frame[...] = move_tokens(2, in_plane_wide[...])
     arrive(grad_z)
     vt_grad_frame[...] = move_tokens(3, in_z[0])
+    column_copies[2] = start_columns(2, vt_grad_frame[...])
     mixed_grad[...] = (cot_frame[...].astype(F32) + dot(vt_grad_frame[...], weights[2])).astype(BF16)
     feature_copies[1] = start_features(1, mixed_grad)
     as_grad[...] = dot_nt(mixed_grad[...], weights[1]).astype(BF16)
     vs_grad[...] = attend_values_back(chance_s, as_grad).astype(BF16)
     column_copies[0] = start_columns(0, vs_grad[...])
-    column_copies[2] = start_columns(2, vt_grad_frame[...])
-
-    arrive([feature_copies[0], feature_copies[1], column_copies[0], column_copies[1]])
-    first_s = first_ring(0)
+
+    arrive([feature_copies[1], feature_copies[2], column_copies[1], column_copies[2]])
+    first_x = first_ring(0)
     arrive(value_z)
     value_t[...] = in_z[1]
     attended_t[...] = attend(chance_t, value_t).astype(BF16)
     column_copies[3] = start_columns(3, attended_t[...])
-    arrive([feature_copies[2], feature_copies[3], column_copies[2], column_copies[3]])
-    first_t = first_ring(1)
-    first_relay(0, first_s)
+    arrive([feature_copies[0], feature_copies[3], column_copies[0], column_copies[3]])
+    first_y = first_ring(1)
+    first_relay(0, first_x)
     query_part, key_part = attend_scores_back(chance_s, sq, sk, value_s, as_grad)
     sq_grad[...] = query_part.astype(BF16).T
     sk_grad[...] = key_part.astype(BF16).T
-    first_relay(1, first_t)
+    first_relay(1, first_y)
     input_grad[...] = (mixed_grad[...].astype(F32) + dot(vs_grad[...], weights[0])).astype(BF16)
     query_part, key_part = attend_scores_back(chance_t, tq, tk, value_t, at_grad)
     rows_one[...] = query_part
@@ -472,16 +507,12 @@
     split_pairs(rows_one, tq_grad)
     split_pairs(rows_two, tk_grad)
 
-    first_end(0, first_s)
-    second_s = second_ring(0)
-    first_end(1, first_t)
-    second_t = second_ring(1)
-    second_relay(0, second_s)
-    second_relay(1, second_t)
-    last_s = second_end(0, second_s)
-    last_t = second_end(1, second_t)
-    finish(0, last_s)
-    finish(1, last_t)
+    first_end(0, first_x)
+    second_y = second_ring(0)
+    first_end(1, first_y)
+    second_x = second_ring(1)
+    last = last_line([second_end(0, second_y), second_end(1, second_x)])
+    finish(last)
     for copy in sent:
         copy.wait_send()
 
@@ -518,14 +549,16 @@
         pltpu.VMEM((4, WIDTH, 2 * TOKENS), BF16),
         pltpu.VMEM((4, 2, 2 * TOKENS, LANES), BF16),
         pltpu.VMEM((4, 2, TOKENS, LANES), BF16),
-        pltpu.VMEM((2, 2, 2, 4, ROW_BLOCK, LANES), BF16),
-        pltpu.VMEM((2, 6, 2, ROW_BLOCK, LANES), BF16),
-        pltpu.VMEM((2, 4, ROW_BLOCK, LANES), BF16),
-        pltpu.VMEM((2, 6, CUT, LANES), BF16),
-        pltpu.VMEM((2, 8 * SHARE_ROWS, LANES), BF16),
-        pltpu.VMEM((2, 7, SHARE_ROWS, LANES), BF16),
+        pltpu.VMEM((2, 4, PIECE, 128), BF16),
+        pltpu.VMEM((2, 6, PIECE - CUT, 128), BF16),
+        pltpu.VMEM((PIECE, 128), F32),
+        pltpu.VMEM((2, 4, BLOCK_ROWS, 128), BF16),
+        pltpu.VMEM((2, 3, BLOCK_ROWS, 128), BF16),
+        pltpu.VMEM((8, SHARE_ROWS, 128), BF16),
+        pltpu.VMEM((7, SHARE_ROWS, 128), BF16),
+        pltpu.VMEM((SHARE_ROWS, 128), F32),
     ]
-    scratch += [dma((14,))] + [dma((3, 7))] * 4 + [dma((4,))] * 4 + [dma((2, 6))] * 4 + [dma((2, 7))] * 2
+    scratch += [dma((15,))] + [dma((3, 7))] * 4 + [dma((4,))] * 4 + [dma((2, 6))] * 2 + [dma((2, 3))] * 2 + [dma((7,))] * 2
     results = [
         jax.ShapeDtypeStruct(wide, BF16),
         jax.ShapeDtypeStruct((INNER, TOKENS), BF16),

time: 70.1 us -> 65.1 us (0.929)
  Pallas kernels: 69.4 us -> 64.3 us
    pallas_call x1, Pallas kernels: 67.2 us -> 62.1 us  [body(): pl.pallas_call(functools.partial(kernel, grad_scale), out_shape=results,...]
where the time goes in v5:
time: 65.1 us; the launch traced here: 65 us
  Pallas kernels  64.3 us (99%)
    pallas_call x1, Pallas kernels, body(): pl.pallas_call(functools.partial(kernel, grad_scale), out_shape=results,...  62.1 us
    pallas_call x1, Pallas kernels, body(): pl.pallas_call(hand_over, out_shape=results, in_specs=[pl.BlockSpec(memor...  2.2 us

profile of v5, /device:TPU:4, one launch (start us, length us, event | category | flops | bytes accessed | tf_op | source)
XLA Modules:
  0.0 65.0 jit_solution(17304506329052358661)
XLA Ops:
  0.6 62.1 %block_backward.1 = (bf16[128,1152]{1,0:T(8,128)(2,1)}, bf16[576,128]{1,0:T(8,128)(2,1)}, bf16[576,128]{1,0:T(8,128)(2,1)}, bf16[64,2,576]{2,1,0:T(2,128)(2,1)},...) custom-call(bf16[128,1152]{1,0:T(8,128)(2,1)} %bitcast.22, bf16[576,128]{1,0:T(8,128)(2,1)} %bitcast.26, ...), custom_call_target="tpu_custom_call" | custom-call | tf_op jit(solution)/shard_map/block_backward/pallas_call | solution.py:570
  62.8 2.2 %hand_over.1 = (bf16[128,1152]{1,0:T(8,128)(2,1)}, bf16[576,128]{1,0:T(8,128)(2,1)}, bf16[576,128]{1,0:T(8,128)(2,1)}, bf16[64,2,576]{2,1,0:T(2,128)(2,1)}, bf16...) custom-call(bf16[128,1152]{1,0:T(8,128)(2,1)} %get-tuple-element.18.refs_0_, bf16[576,128]{1,0:T(8,128)(2,1)} %get-tuple-element.19.refs_1_, ...), custom_call_target="tpu_custom_call" | custom-call | tf_op jit(solution)/shard_map/hand_over/pallas_call | solution.py:581

commit v6 on v5

--- a/solution.py
+++ b/solution.py
@@ -16,12 +16,12 @@
 FRAMES = 64
 SCORE_SCALE = HEAD_DIM ** (-0.5)
 ROW_BLOCK = 144
-LANES = 384
-PIECE = 9 * ROW_BLOCK
-CUT = 640
+LANES = 256
+PIECE = 4 * ROW_BLOCK + 80
+CUT = 336
 BLOCK_ROWS = 2 * ROW_BLOCK + 48
 SHARE_ROWS = 96
-PAIRS = ((1, 2), (0, 3))
+PAIRS = ((1, 3), (2, 0))
 F32 = jnp.float32
 BF16 = jnp.bfloat16
 MESH = pl.DeviceIdType.MESH
@@ -54,12 +54,11 @@
             for y in range(2)
         ]
     )
-    picks = np.zeros((2, 2, 2, INNER, LANES), np.float32)
+    picks = np.zeros((2, 2, INNER, LANES), np.float32)
     for core in range(2):
-        for matrix in range(2):
-            for y_hi in range(2):
-                for column in range(144):
-                    picks[core, matrix, y_hi, (2 * y_hi + core) * 144 + column, matrix * 144 + column] = 1.0
+        for y_hi in range(2):
+            for column in range(144):
+                picks[core, y_hi, (2 * y_hi + core) * 144 + column, column] = 1.0
     share_moves = one_hot(
         [
             part * 144 + z * 18 + r if part < 4 else -1
@@ -210,7 +209,7 @@
         ]
     ):
         copy = pltpu.make_async_copy(source, target, load_sem.at[number])
-        if number < 11:
+        if number < 3:
             copy.start()
         loads.append(copy)
 
@@ -278,84 +277,86 @@
 
     def start_columns(number, rows):
         for side in range(2):
-            place = 0 if number < 2 else 1
-            picked[number, side, 0:TOKENS, :] = dot(rows, picks[core, place, side]).astype(BF16)
-            picked_out[number, side] = dot(rows, picks[1 - core, place, side]).astype(BF16)
+            picked[number, side, 0:TOKENS, :] = dot(rows, picks[core, side]).astype(BF16)
+            picked_out[number, side] = dot(rows, picks[1 - core, side]).astype(BF16)
         return send(
             picked_out.at[number], picked.at[number, :, TOKENS : 2 * TOKENS],
             picked_send.at[number], picked_recv.at[number], sibling,
         )
 
-    def make_pieces(pair, to):
+    places = (x, y)
+    rings = (along_x, along_y)
+    ring_of = {number: ring for ring, numbers in enumerate(PAIRS) for number in numbers}
+    slot_half = (0, 1, 1, 0, 0, 1)
+
+    def make_pieces(number, to):
         rests = None
         for sub in range(4):
-            side, y_lo_at, x_at = (sub // 2, sub % 2, to) if pair == 0 else (to // 2, to % 2, sub)
+            side, y_lo_at, x_at = (sub // 2, sub % 2, to) if ring_of[number] == 0 else (to // 2, to % 2, sub)
             rows = pl.ds(pl.multiple_of((y_lo_at * 4 + x_at) * ROW_BLOCK, 16), ROW_BLOCK)
-            one, two = PAIRS[pair]
-            total = dot(factors[one, rows, :], picked[one, side]) + dot(factors[two, rows, :], picked[two, side])
-            at = 2 * sub * ROW_BLOCK
-            sums[pair, to, at : at + ROW_BLOCK, :] = total[:, 0:128].astype(BF16)
-            sums[pair, to, at + ROW_BLOCK : at + 2 * ROW_BLOCK, :] = total[:, 128:256].astype(BF16)
-            rest = total[:, 256:384]
-            rests = rest if sub == 0 else rests + pltpu.roll(rest, 32 * sub, 1)
-        sums[pair, to, 8 * ROW_BLOCK : PIECE, :] = rests.astype(BF16)
-
-    def piece(pair, to, half):
-        return sums.at[pair, to, 0:CUT] if half == 0 else sums.at[pair, to, CUT:PIECE]
-
-    slot_half = (0, 1, 1, 0, 0, 1)
-
-    def slot_ref(pair, slot):
-        return arrived.at[pair, slot, 0 : (CUT if slot_half[slot] == 0 else PIECE - CUT)]
-
-    places = (x, y)
-    rings = (along_x, along_y)
-
-    def ring_copy(pair, slot, source):
-        peer = rings[pair](1 if slot % 2 == 0 else -1 + 4)
-        return send(source, slot_ref(pair, slot), ring_send.at[pair, slot], ring_recv.at[pair, slot], peer)
-
-    def first_ring(pair):
-        place = places[pair]
+            total = dot(factors[number, rows, :], picked[number, side])
+            sums[number, to, sub * ROW_BLOCK : (sub + 1) * ROW_BLOCK, :] = total[:, 0:128].astype(BF16)
+            rest = total[:, 128:256]
+            rests = rest if sub == 0 else rests + pltpu.roll(rest, 16 * sub, 1)
+        beside = jnp.concatenate([pltpu.roll(rests[80:ROW_BLOCK], 64, 1), jnp.zeros((16, 128), F32)], axis=0)
+        sums[number, to, 4 * ROW_BLOCK : PIECE, :] = (rests[0:80] + beside).astype(BF16)
+
+    def piece(number, to, half):
+        return sums.at[number, to, 0:CUT] if half == 0 else sums.at[number, to, CUT:PIECE]
+
+    def slot_ref(number, slot):
+        return arrived.at[number, slot, 0 : (CUT if slot_half[slot] == 0 else PIECE - CUT)]
+
+    def ring_copy(number, slot, source):
+        peer = rings[ring_of[number]](1 if slot % 2 == 0 else 3)
+        return send(source, slot_ref(number, slot), ring_send.at[number, slot], ring_recv.at[number, slot], peer)
+
+    def first_ring(number):
+        place = places[ring_of[number]]
         after, across, before = (place + 1) % 4, (place + 2) % 4, (place + 3) % 4
         copies = {}
-        make_pieces(pair, across)
-        copies[0] = ring_copy(pair, 0, piece(pair, across, 0))
-        copies[1] = ring_copy(pair, 1, piece(pair, across, 1))
-        make_pieces(pair, after)
-        copies[2] = ring_copy(pair, 2, piece(pair, after, 1))
-        make_pieces(pair, before)
-        copies[3] = ring_copy(pair, 3, piece(pair, before, 0))
-        make_pieces(pair, place)
+        make_pieces(number, across)
+        copies[0] = ring_copy(number, 0, piece(number, across, 0))
+        copies[1] = ring_copy(number, 1, piece(number, across, 1))
+        make_pieces(number, after)
+        copies[2] = ring_copy(number, 2, piece(number, after, 1))
+        make_pieces(number, before)
+        copies[3] = ring_copy(number, 3, piece(number, before, 0))
+        make_pieces(number, place)
         return copies
 
-    def first_relay(pair, copies):
-        place = places[pair]
+    def first_relay(number, copies):
+        place = places[ring_of[number]]
         after, before = (place + 1) % 4, (place + 3) % 4
         for slot, to, half in ((0, after, 0), (1, before, 1)):
             copies[slot].wait_recv()
-            ref = piece(pair, to, half)
-            ref[...] = (ref[...].astype(F32) + slot_ref(pair, slot)[...].astype(F32)).astype(BF16)
-            copies[slot + 4] = ring_copy(pair, slot + 4, ref)
-
-    lane_group = lax.broadcasted_iota(jnp.int32, (16, 128), 1) // 32
+            ref = piece(number, to, half)
+            ref[...] = (ref[...].astype(F32) + slot_ref(number, slot)[...].astype(F32)).astype(BF16)
+            copies[slot + 4] = ring_copy(number, slot + 4, ref)
+
+    lane_group = lax.broadcasted_iota(jnp.int32, (16, 128), 1) // 16
 
     def first_end(pair, copies):
-        for half, slots in ((0, (3, 4)), (1, (2, 5))):
-            total = piece(pair, places[pair], half)[...].astype(F32)
-            for slot in slots:
-                copies[slot].wait_recv()
-                total += slot_ref(pair, slot)[...].astype(F32)
-            total_one[(0 if half == 0 else CUT) : (CUT if half == 0 else PIECE), :] = total
+        for place, number in enumerate(PAIRS[pair]):
+            for half, slots in ((0, (3, 4)), (1, (2, 5))):
+                total = piece(number, places[pair], half)[...].astype(F32)
+                for slot in slots:
+                    copies[number][slot].wait_recv()
+                    total += slot_ref(number, slot)[...].astype(F32)
+                total_one[place, (0 if half == 0 else CUT) : (CUT if half == 0 else PIECE), :] = total
+            for sub in range(4):
+                sums_two[pair, sub, place * ROW_BLOCK : (place + 1) * ROW_BLOCK, :] = total_one[
+                    place, sub * ROW_BLOCK : (sub + 1) * ROW_BLOCK, :
+                ].astype(BF16)
         for sub in range(4):
-            at = 2 * sub * ROW_BLOCK
-            sums_two[pair, sub, 0 : 2 * ROW_BLOCK, :] = total_one[at : at + 2 * ROW_BLOCK, :].astype(BF16)
             for tile in range(3):
                 packed = jnp.zeros((16, 128), F32)
-                for group in range(4 if tile < 2 else 1):
-                    start = 8 * ROW_BLOCK + 16 * (4 * tile + group)
-                    rest = pltpu.roll(total_one[start : start + 16, :], 32 * ((group - sub) % 4), 1)
-                    packed = jnp.where(lane_group == group, rest, packed)
+                for group in range(4 * tile, min(4 * tile + 4, 9)):
+                    for place in range(2):
+                        start = 4 * ROW_BLOCK + 16 * (group % 5)
+                        turn = (32 * (group % 4) + 16 * place - 16 * sub - (64 if group >= 5 else 0)) % 128
+                        rest = pltpu.roll(total_one[place, start : start + 16, :], turn, 1)
+                        packed = jnp.where(lane_group == 2 * (group % 4) + place, rest, packed)
                 start = 2 * ROW_BLOCK + 16 * tile
                 sums_two[pair, sub, start : start + 16, :] = packed.astype(BF16)
 
@@ -409,15 +410,13 @@
             copies[step - 1].wait_recv()
             total += shares_in[step - 1].astype(F32)
         total_share[...] = total * grad_scale
-        for pair, (one, two) in enumerate(PAIRS):
-            left = total_share[36 * pair : 36 * pair + 18, :]
-            right = total_share[36 * pair + 18 : 36 * pair + 36, :]
-            weight_grads[:, one, 0:128] = left
-            weight_grads[:, one, 128:144] = right[:, 0:16]
-            weight_grads[:, two, 0:112] = right[:, 16:128]
-            for half in range(2):
-                start = 64 * pair + 32 * half
-                weight_grads[9 * half : 9 * half + 9, two, 112:144] = total_share[80:89, start : start + 32]
+        for pair, numbers in enumerate(PAIRS):
+            for place, number in enumerate(numbers):
+                start = 36 * pair + 18 * place
+                weight_grads[:, number, 0:128] = total_share[start : start + 18, :]
+                for half in range(2):
+                    lane = 64 * pair + 32 * half + 16 * place
+                    weight_grads[9 * half : 9 * half + 9, number, 128:144] = total_share[80:89, lane : lane + 16]
 
     def join_pairs(pairs, rows):
         for frame in range(FRAMES):
@@ -429,6 +428,8 @@
             pairs[frame] = rows[line_order(frame), :].astype(BF16)
 
     loads[0].wait()
+    for copy in loads[3:11]:
+        copy.start()
     cot[...] = join_pairs(cot_pairs, rows_wide)
     pl.semaphore_wait(barrier, len(greeted))
     cot_z = start_z(0, cot, in_z_wide)
@@ -474,32 +475,39 @@
     out_z[1] = move_tokens(4, in_plane[1])
     value_z = start_z(2, out_z.at[1], in_z.at[1])
     feature_copies[2] = start_features(2, mixed)
-    feature_copies[3] = start_features(3, cot)
-
-    arrive(cot_plane)
-    cot_frame[...] = move_tokens(2, in_plane_wide[...])
+
+    rings_at = {}
+
+    def ready(number):
+        arrive([feature_copies[number], column_copies[number]])
+        rings_at[number] = first_ring(number)
+
     arrive(grad_z)
     vt_grad_frame[...] = move_tokens(3, in_z[0])
     column_copies[2] = start_columns(2, vt_grad_frame[...])
+    feature_copies[3] = start_features(3, cot)
+    ready(2)
+    arrive(cot_plane)
+    cot_frame[...] = move_tokens(2, in_plane_wide[...])
     mixed_grad[...] = (cot_frame[...].astype(F32) + dot(vt_grad_frame[...], weights[2])).astype(BF16)
     feature_copies[1] = start_features(1, mixed_grad)
     as_grad[...] = dot_nt(mixed_grad[...], weights[1]).astype(BF16)
     vs_grad[...] = attend_values_back(chance_s, as_grad).astype(BF16)
     column_copies[0] = start_columns(0, vs_grad[...])
-
-    arrive([feature_copies[1], feature_copies[2], column_copies[1], column_copies[2]])
-    first_x = first_ring(0)
+    ready(1)
+    first_relay(2, rings_at[2])
+    ready(0)
     arrive(value_z)
     value_t[...] = in_z[1]
     attended_t[...] = attend(chance_t, value_t).astype(BF16)
     column_copies[3] = start_columns(3, attended_t[...])
-    arrive([feature_copies[0], feature_copies[3], column_copies[0], column_copies[3]])
-    first_y = first_ring(1)
-    first_relay(0, first_x)
+    first_relay(1, rings_at[1])
+    ready(3)
+    first_relay(0, rings_at[0])
     query_part, key_part = attend_scores_back(chance_s, sq, sk, value_s, as_grad)
     sq_grad[...] = query_part.astype(BF16).T
     sk_grad[...] = key_part.astype(BF16).T
-    first_relay(1, first_y)
+    first_relay(3, rings_at[3])
     input_grad[...] = (mixed_grad[...].astype(F32) + dot(vs_grad[...], weights[0])).astype(BF16)
     query_part, key_part = attend_scores_back(chance_t, tq, tk, value_t, at_grad)
     rows_one[...] = query_part
@@ -507,10 +515,10 @@
     split_pairs(rows_one, tq_grad)
     split_pairs(rows_two, tk_grad)
 
-    first_end(0, first_x)
+    first_end(1, rings_at)
+    second_x = second_ring(1)
+    first_end(0, rings_at)
     second_y = second_ring(0)
-    first_end(1, first_y)
-    second_x = second_ring(1)
     last = last_line([second_end(0, second_y), second_end(1, second_x)])
     finish(last)
     for copy in sent:
@@ -549,16 +557,16 @@
         pltpu.VMEM((4, WIDTH, 2 * TOKENS), BF16),
         pltpu.VMEM((4, 2, 2 * TOKENS, LANES), BF16),
         pltpu.VMEM((4, 2, TOKENS, LANES), BF16),
-        pltpu.VMEM((2, 4, PIECE, 128), BF16),
-        pltpu.VMEM((2, 6, PIECE - CUT, 128), BF16),
-        pltpu.VMEM((PIECE, 128), F32),
+        pltpu.VMEM((4, 4, PIECE, 128), BF16),
+        pltpu.VMEM((4, 6, CUT, 128), BF16),
+        pltpu.VMEM((2, PIECE, 128), F32),
         pltpu.VMEM((2, 4, BLOCK_ROWS, 128), BF16),
         pltpu.VMEM((2, 3, BLOCK_ROWS, 128), BF16),
         pltpu.VMEM((8, SHARE_ROWS, 128), BF16),
         pltpu.VMEM((7, SHARE_ROWS, 128), BF16),
         pltpu.VMEM((SHARE_ROWS, 128), F32),
     ]
-    scratch += [dma((15,))] + [dma((3, 7))] * 4 + [dma((4,))] * 4 + [dma((2, 6))] * 2 + [dma((2, 3))] * 2 + [dma((7,))] * 2
+    scratch += [dma((15,))] + [dma((3, 7))] * 4 + [dma((4,))] * 4 + [dma((4, 6))] * 2 + [dma((2, 3))] * 2 + [dma((7,))] * 2
     results = [
         jax.ShapeDtypeStruct(wide, BF16),
         jax.ShapeDtypeStruct((INNER, TOKENS), BF16),

time: 65.1 us -> 63.3 us (0.972)
  Pallas kernels: 64.3 us -> 61.9 us
    pallas_call x1, Pallas kernels: 62.1 us -> 59.7 us  [body(): pl.pallas_call(functools.partial(kernel, grad_scale), out_shape=results,...]
where the time goes in v6:
time: 63.3 us; the launch traced here: 62.6 us
  Pallas kernels  61.9 us (98%)
  between operations  0.64 us (1%)
    pallas_call x1, Pallas kernels, body(): pl.pallas_call(functools.partial(kernel, grad_scale), out_shape=results,...  59.7 us
    pallas_call x1, Pallas kernels, body(): pl.pallas_call(hand_over, out_shape=results, in_specs=[pl.BlockSpec(memor...  2.2 us

profile of v6, /device:TPU:4, one launch (start us, length us, event | category | flops | bytes accessed | tf_op | source)
XLA Modules:
  0.0 62.6 jit_solution(9853234917431390583)
XLA Ops:
  0.6 59.7 %block_backward.1 = (bf16[128,1152]{1,0:T(8,128)(2,1)}, bf16[576,128]{1,0:T(8,128)(2,1)}, bf16[576,128]{1,0:T(8,128)(2,1)}, bf16[64,2,576]{2,1,0:T(2,128)(2,1)},...) custom-call(bf16[128,1152]{1,0:T(8,128)(2,1)} %bitcast.22, bf16[576,128]{1,0:T(8,128)(2,1)} %bitcast.26, ...), custom_call_target="tpu_custom_call" | custom-call | tf_op jit(solution)/shard_map/block_backward/pallas_call | solution.py:578
  60.4 2.2 %hand_over.1 = (bf16[128,1152]{1,0:T(8,128)(2,1)}, bf16[576,128]{1,0:T(8,128)(2,1)}, bf16[576,128]{1,0:T(8,128)(2,1)}, bf16[64,2,576]{2,1,0:T(2,128)(2,1)}, bf16...) custom-call(bf16[128,1152]{1,0:T(8,128)(2,1)} %get-tuple-element.18.refs_0_, bf16[576,128]{1,0:T(8,128)(2,1)} %get-tuple-element.19.refs_1_, ...), custom_call_target="tpu_custom_call" | custom-call | tf_op jit(solution)/shard_map/hand_over/pallas_call | solution.py:589

commit v7 on v6

--- a/solution.py
+++ b/solution.py
@@ -19,8 +19,8 @@
 LANES = 256
 PIECE = 4 * ROW_BLOCK + 80
 CUT = 336
-BLOCK_ROWS = 2 * ROW_BLOCK + 48
-SHARE_ROWS = 96
+BLOCK_ROWS = ROW_BLOCK + 32
+SHARE_ROWS = 32
 PAIRS = ((1, 3), (2, 0))
 F32 = jnp.float32
 BF16 = jnp.bfloat16
@@ -60,22 +60,17 @@
             for column in range(144):
                 picks[core, y_hi, (2 * y_hi + core) * 144 + column, column] = 1.0
     share_moves = one_hot(
-        [
-            part * 144 + z * 18 + r if part < 4 else -1
-            for z in range(8)
-            for part, r in [divmod(row, 18) for row in range(80)]
-        ],
-        4 * ROW_BLOCK,
+        [z * 18 + row if row < 18 else -1 for z in range(8) for row in range(SHARE_ROWS)], ROW_BLOCK
     )
     rest_moves = []
-    for group in range(4):
+    for group in range(2):
         source = []
         for z in range(8):
-            for row in range(16):
-                at = z * 18 + 9 * (group % 2) + row
-                place, turn = at // 16, (group - at // 16) % 4
-                source.append(turn * 48 + place // 4 * 16 + at % 16 if row < 9 else -1)
-        rest_moves.append(one_hot(source, 192))
+            for row in range(SHARE_ROWS):
+                at = z * 18 + 9 * group + row - 18
+                place, turn = at // 16, (group - at // 16) % 8
+                source.append(turn * 32 + place // 8 * 16 + at % 16 if 18 <= row < 27 else -1)
+        rest_moves.append(one_hot(source, 256))
     tables = (token_moves, feature_moves, picks, share_moves, np.stack(rest_moves))
     return [jnp.asarray(table, BF16) for table in tables]
 
@@ -335,88 +330,77 @@
             copies[slot + 4] = ring_copy(number, slot + 4, ref)
 
     lane_group = lax.broadcasted_iota(jnp.int32, (16, 128), 1) // 16
-
-    def first_end(pair, copies):
-        for place, number in enumerate(PAIRS[pair]):
-            for half, slots in ((0, (3, 4)), (1, (2, 5))):
-                total = piece(number, places[pair], half)[...].astype(F32)
-                for slot in slots:
-                    copies[number][slot].wait_recv()
-                    total += slot_ref(number, slot)[...].astype(F32)
-                total_one[place, (0 if half == 0 else CUT) : (CUT if half == 0 else PIECE), :] = total
-            for sub in range(4):
-                sums_two[pair, sub, place * ROW_BLOCK : (place + 1) * ROW_BLOCK, :] = total_one[
-                    place, sub * ROW_BLOCK : (sub + 1) * ROW_BLOCK, :
-                ].astype(BF16)
+    share_group = lax.broadcasted_iota(jnp.int32, (8 * SHARE_ROWS, 128), 1) // 16
+
+    def second_place(number):
+        return places[1 - ring_of[number]]
+
+    def second_line(number):
+        copies = rings_at[number]
+        for half, slots in ((0, (3, 4)), (1, (2, 5))):
+            total = piece(number, places[ring_of[number]], half)[...].astype(F32)
+            for slot in slots:
+                copies[slot].wait_recv()
+                total += slot_ref(number, slot)[...].astype(F32)
+            total_one[(0 if half == 0 else CUT) : (CUT if half == 0 else PIECE), :] = total
         for sub in range(4):
-            for tile in range(3):
+            sums_two[number, sub, 0:ROW_BLOCK, :] = total_one[sub * ROW_BLOCK : (sub + 1) * ROW_BLOCK, :].astype(BF16)
+            for tile in range(2):
                 packed = jnp.zeros((16, 128), F32)
-                for group in range(4 * tile, min(4 * tile + 4, 9)):
-                    for place in range(2):
-                        start = 4 * ROW_BLOCK + 16 * (group % 5)
-                        turn = (32 * (group % 4) + 16 * place - 16 * sub - (64 if group >= 5 else 0)) % 128
-                        rest = pltpu.roll(total_one[place, start : start + 16, :], turn, 1)
-                        packed = jnp.where(lane_group == 2 * (group % 4) + place, rest, packed)
-                start = 2 * ROW_BLOCK + 16 * tile
-                sums_two[pair, sub, start : start + 16, :] = packed.astype(BF16)
-
-    def second_ring(pair):
-        place = places[1 - pair]
-        copies = []
+                for group in range(8) if tile == 0 else (8,):
+                    start = 4 * ROW_BLOCK + 16 * (group % 5)
+                    turn = (16 * (group % 8) - 16 * sub - (64 if group >= 5 else 0)) % 128
+                    rest = total_one[start : start + 16, :]
+                    rest = pltpu.roll(rest, turn, 1) if turn else rest
+                    packed = jnp.where(lane_group == group % 8, rest, packed)
+                start = ROW_BLOCK + 16 * tile
+                sums_two[number, sub, start : start + 16, :] = packed.astype(BF16)
+        seconds[number] = [
+            send(
+                sums_two.at[number, (second_place(number) + step) % 4], arrived_two.at[number, step - 1],
+                ring_two_send.at[number, step - 1], ring_two_recv.at[number, step - 1],
+                rings[1 - ring_of[number]](step),
+            )
+            for step in range(1, 4)
+        ]
+
+    def third_line(number):
+        total = sums_two[number, second_place(number)].astype(F32)
         for step in range(1, 4):
-            copies.append(
-                send(
-                    sums_two.at[pair, (place + step) % 4], arrived_two.at[pair, step - 1],
-                    ring_two_send.at[pair, step - 1], ring_two_recv.at[pair, step - 1], rings[1 - pair](step),
-                )
+            seconds[number][step - 1].wait_recv()
+            total += arrived_two[number, step - 1].astype(F32)
+        moved = dot(share_moves[...], total[0:ROW_BLOCK].astype(BF16))
+        ends = total[ROW_BLOCK:BLOCK_ROWS]
+        turned = [ends] + [pltpu.roll(ends, 16 * turn, 1) for turn in range(1, 8)]
+        turned = jnp.concatenate(turned, axis=0).astype(BF16)
+        for group in range(2):
+            moved += jnp.where(share_group == group, dot(rest_moves[group], turned), 0.0)
+        moved = moved.astype(BF16)
+        for z_at in range(8):
+            shares[number, z_at] = moved[SHARE_ROWS * z_at : SHARE_ROWS * (z_at + 1)]
+        thirds[number] = [
+            send(
+                shares.at[number, (z + step) % 8], shares_in.at[number, step - 1],
+                share_send.at[number, step - 1], share_recv.at[number, step - 1], along_z(step),
             )
-        return copies
-
-    def second_end(pair, copies):
-        total = sums_two[pair, places[1 - pair]].astype(F32)
-        for step in range(1, 4):
-            copies[step - 1].wait_recv()
-            total += arrived_two[pair, step - 1].astype(F32)
-        return total
-
-    def last_line(totals):
-        whole = jnp.concatenate([total[0 : 2 * ROW_BLOCK] for total in totals], axis=0).astype(BF16)
-        moved = dot(share_moves[...], whole).astype(BF16)
-        rest = jnp.zeros((TOKENS, 128), F32)
-        lanes = lax.broadcasted_iota(jnp.int32, (TOKENS, 128), 1) // 32
-        for pair, total in enumerate(totals):
-            ends = total[2 * ROW_BLOCK : BLOCK_ROWS]
-            turned = [ends] + [pltpu.roll(ends, 32 * turn, 1) for turn in range(1, 4)]
-            turned = jnp.concatenate(turned, axis=0).astype(BF16)
-            for group in (2 * pair, 2 * pair + 1):
-                rest = jnp.where(lanes == group, dot(rest_moves[group], turned), rest)
-        rest = rest.astype(BF16)
-        for z_at in range(8):
-            shares[z_at, 0:80, :] = moved[80 * z_at : 80 * z_at + 80]
-            shares[z_at, 80:96, :] = rest[16 * z_at : 16 * z_at + 16]
-        copies = []
+            for step in range(1, 8)
+        ]
+
+    def finish(number):
+        total = shares[number, z].astype(F32)
         for step in range(1, 8):
-            copies.append(
-                send(
-                    shares.at[(z + step) % 8], shares_in.at[step - 1],
-                    share_send.at[step - 1], share_recv.at[step - 1], along_z(step),
-                )
-            )
-        return copies
-
-    def finish(copies):
-        total = shares[z].astype(F32)
-        for step in range(1, 8):
-            copies[step - 1].wait_recv()
-            total += shares_in[step - 1].astype(F32)
+            thirds[number][step - 1].wait_recv()
+            total += shares_in[number, step - 1].astype(F32)
         total_share[...] = total * grad_scale
-        for pair, numbers in enumerate(PAIRS):
-            for place, number in enumerate(numbers):
-                start = 36 * pair + 18 * place
-                weight_grads[:, number, 0:128] = total_share[start : start + 18, :]
-                for half in range(2):
-                    lane = 64 * pair + 32 * half + 16 * place
-                    weight_grads[9 * half : 9 * half + 9, number, 128:144] = total_share[80:89, lane : lane + 16]
+        weight_grads[:, number, 0:128] = total_share[0:18, :]
+        for half in range(2):
+            weight_grads[9 * half : 9 * half + 9, number, 128:144] = total_share[18:27, 16 * half : 16 * half + 16]
+
+    rings_at, seconds, thirds = {}, {}, {}
+
+    def ready(number):
+        arrive([feature_copies[number], column_copies[number]])
+        rings_at[number] = first_ring(number)
 
     def join_pairs(pairs, rows):
         for frame in range(FRAMES):
@@ -476,51 +460,48 @@
     value_z = start_z(2, out_z.at[1], in_z.at[1])
     feature_copies[2] = start_features(2, mixed)
 
-    rings_at = {}
-
-    def ready(number):
-        arrive([feature_copies[number], column_copies[number]])
-        rings_at[number] = first_ring(number)
-
+    feature_copies[3] = start_features(3, cot)
     arrive(grad_z)
     vt_grad_frame[...] = move_tokens(3, in_z[0])
     column_copies[2] = start_columns(2, vt_grad_frame[...])
-    feature_copies[3] = start_features(3, cot)
-    ready(2)
     arrive(cot_plane)
     cot_frame[...] = move_tokens(2, in_plane_wide[...])
     mixed_grad[...] = (cot_frame[...].astype(F32) + dot(vt_grad_frame[...], weights[2])).astype(BF16)
     feature_copies[1] = start_features(1, mixed_grad)
+    ready(2)
     as_grad[...] = dot_nt(mixed_grad[...], weights[1]).astype(BF16)
     vs_grad[...] = attend_values_back(chance_s, as_grad).astype(BF16)
     column_copies[0] = start_columns(0, vs_grad[...])
     ready(1)
-    first_relay(2, rings_at[2])
-    ready(0)
     arrive(value_z)
     value_t[...] = in_z[1]
     attended_t[...] = attend(chance_t, value_t).astype(BF16)
     column_copies[3] = start_columns(3, attended_t[...])
+    first_relay(2, rings_at[2])
+    ready(0)
+    ready(3)
     first_relay(1, rings_at[1])
-    ready(3)
+    input_grad[...] = (mixed_grad[...].astype(F32) + dot(vs_grad[...], weights[0])).astype(BF16)
     first_relay(0, rings_at[0])
     query_part, key_part = attend_scores_back(chance_s, sq, sk, value_s, as_grad)
     sq_grad[...] = query_part.astype(BF16).T
     sk_grad[...] = key_part.astype(BF16).T
     first_relay(3, rings_at[3])
-    input_grad[...] = (mixed_grad[...].astype(F32) + dot(vs_grad[...], weights[0])).astype(BF16)
+    second_line(2)
     query_part, key_part = attend_scores_back(chance_t, tq, tk, value_t, at_grad)
     rows_one[...] = query_part
     rows_two[...] = key_part
     split_pairs(rows_one, tq_grad)
     split_pairs(rows_two, tk_grad)
-
-    first_end(1, rings_at)
-    second_x = second_ring(1)
-    first_end(0, rings_at)
-    second_y = second_ring(0)
-    last = last_line([second_end(0, second_y), second_end(1, second_x)])
-    finish(last)
+    second_line(1)
+    third_line(2)
+    second_line(0)
+    third_line(1)
+    second_line(3)
+    third_line(0)
+    third_line(3)
+    for number in (2, 1, 0, 3):
+        finish(number)
     for copy in sent:
         copy.wait_send()
 
@@ -559,14 +540,14 @@
         pltpu.VMEM((4, 2, TOKENS, LANES), BF16),
         pltpu.VMEM((4, 4, PIECE, 128), BF16),
         pltpu.VMEM((4, 6, CUT, 128), BF16),
-        pltpu.VMEM((2, PIECE, 128), F32),
-        pltpu.VMEM((2, 4, BLOCK_ROWS, 128), BF16),
-        pltpu.VMEM((2, 3, BLOCK_ROWS, 128), BF16),
-        pltpu.VMEM((8, SHARE_ROWS, 128), BF16),
-        pltpu.VMEM((7, SHARE_ROWS, 128), BF16),
+        pltpu.VMEM((PIECE, 128), F32),
+        pltpu.VMEM((4, 4, BLOCK_ROWS, 128), BF16),
+        pltpu.VMEM((4, 3, BLOCK_ROWS, 128), BF16),
+        pltpu.VMEM((4, 8, SHARE_ROWS, 128), BF16),
+        pltpu.VMEM((4, 7, SHARE_ROWS, 128), BF16),
         pltpu.VMEM((SHARE_ROWS, 128), F32),
     ]
-    scratch += [dma((15,))] + [dma((3, 7))] * 4 + [dma((4,))] * 4 + [dma((4, 6))] * 2 + [dma((2, 3))] * 2 + [dma((7,))] * 2
+    scratch += [dma((15,))] + [dma((3, 7))] * 4 + [dma((4,))] * 4 + [dma((4, 6))] * 2 + [dma((4, 3))] * 2 + [dma((4, 7))] * 2
     results = [
         jax.ShapeDtypeStruct(wide, BF16),
         jax.ShapeDtypeStruct((INNER, TOKENS), BF16),

time: 63.3 us -> 61.5 us (0.972)
  Pallas kernels: 61.9 us -> 59.7 us
    pallas_call x1, Pallas kernels: 59.7 us -> 57.5 us  [body(): pl.pallas_call(functools.partial(kernel, grad_scale), out_shape=results,...]
where the time goes in v7:
time: 61.5 us; the launch traced here: 60.3 us
  Pallas kernels  59.7 us (97%)
  between operations  0.64 us (1%)
    pallas_call x1, Pallas kernels, body(): pl.pallas_call(functools.partial(kernel, grad_scale), out_shape=results,...  57.5 us
    pallas_call x1, Pallas kernels, body(): pl.pallas_call(hand_over, out_shape=results, in_specs=[pl.BlockSpec(memor...  2.2 us

profile of v7, /device:TPU:4, one launch (start us, length us, event | category | flops | bytes accessed | tf_op | source)
XLA Modules:
  0.0 60.3 jit_solution(18180674874877335116)
XLA Ops:
  0.6 57.5 %block_backward.1 = (bf16[128,1152]{1,0:T(8,128)(2,1)}, bf16[576,128]{1,0:T(8,128)(2,1)}, bf16[576,128]{1,0:T(8,128)(2,1)}, bf16[64,2,576]{2,1,0:T(2,128)(2,1)},...) custom-call(bf16[128,1152]{1,0:T(8,128)(2,1)} %bitcast.22, bf16[576,128]{1,0:T(8,128)(2,1)} %bitcast.26, ...), custom_call_target="tpu_custom_call" | custom-call | tf_op jit(solution)/shard_map/block_backward/pallas_call | solution.py:559
  58.1 2.2 %hand_over.1 = (bf16[128,1152]{1,0:T(8,128)(2,1)}, bf16[576,128]{1,0:T(8,128)(2,1)}, bf16[576,128]{1,0:T(8,128)(2,1)}, bf16[64,2,576]{2,1,0:T(2,128)(2,1)}, bf16...) custom-call(bf16[128,1152]{1,0:T(8,128)(2,1)} %get-tuple-element.18.refs_0_, bf16[576,128]{1,0:T(8,128)(2,1)} %get-tuple-element.19.refs_1_, ...), custom_call_target="tpu_custom_call" | custom-call | tf_op jit(solution)/shard_map/hand_over/pallas_call | solution.py:570

commit v8 on v7

--- a/solution.py
+++ b/solution.py
@@ -158,6 +158,7 @@
     grad_scale,
     block_hbm, sq_hbm, sk_hbm, cot_hbm, tq_hbm, tk_hbm, weights_hbm,
     token_moves_hbm, feature_moves_hbm, picks_hbm, share_moves_hbm, rest_moves_hbm,
+    input_grad_hbm, sq_grad_hbm, sk_grad_hbm, tq_grad_hbm, tk_grad_hbm, weight_grads_hbm,
     input_grad, sq_grad, sk_grad, tq_grad, tk_grad, weight_grads,
     block, sq_turned, sk_turned, cot_pairs, tq_pairs, tk_pairs, weights, token_moves, feature_moves, picks, share_moves, rest_moves,
     sq, sk, cot, tq, tk, rows_wide, rows_one, rows_two,
@@ -165,7 +166,7 @@
     mixed, mixed_grad, cot_frame, vt_grad_frame,
     in_z_wide, out_plane_wide, in_plane_wide, out_plane, in_plane, out_z, in_z,
     factors, picked, picked_out, sums, arrived, total_one, sums_two, arrived_two, shares, shares_in, total_share,
-    load_sem, z_send, z_recv, plane_send, plane_recv, factor_send, factor_recv, picked_send, picked_recv,
+    load_sem, store_sem, z_send, z_recv, plane_send, plane_recv, factor_send, factor_recv, picked_send, picked_recv,
     ring_send, ring_recv, ring_two_send, ring_two_recv, share_send, share_recv,
 ):
     dp, seq = lax.axis_index("dp"), lax.axis_index("seq")
@@ -214,7 +215,12 @@
     for peer in greeted:
         pl.semaphore_signal(barrier, inc=1, device_id=peer, device_id_type=MESH)
 
-    sent = []
+    sent, stored = [], []
+
+    def store(source, target):
+        copy = pltpu.make_async_copy(source, target, store_sem.at[len(stored)])
+        copy.start()
+        stored.append(copy)
 
     def send(source, target, send_sem, recv_sem, peer):
         copy = pltpu.make_async_remote_copy(
@@ -469,10 +475,10 @@
     mixed_grad[...] = (cot_frame[...].astype(F32) + dot(vt_grad_frame[...], weights[2])).astype(BF16)
     feature_copies[1] = start_features(1, mixed_grad)
     ready(2)
+    ready(1)
     as_grad[...] = dot_nt(mixed_grad[...], weights[1]).astype(BF16)
     vs_grad[...] = attend_values_back(chance_s, as_grad).astype(BF16)
     column_copies[0] = start_columns(0, vs_grad[...])
-    ready(1)
     arrive(value_z)
     value_t[...] = in_z[1]
     attended_t[...] = attend(chance_t, value_t).astype(BF16)
@@ -482,10 +488,13 @@
     ready(3)
     first_relay(1, rings_at[1])
     input_grad[...] = (mixed_grad[...].astype(F32) + dot(vs_grad[...], weights[0])).astype(BF16)
+    store(input_grad, input_grad_hbm)
     first_relay(0, rings_at[0])
     query_part, key_part = attend_scores_back(chance_s, sq, sk, value_s, as_grad)
     sq_grad[...] = query_part.astype(BF16).T
     sk_grad[...] = key_part.astype(BF16).T
+    store(sq_grad, sq_grad_hbm)
+    store(sk_grad, sk_grad_hbm)
     first_relay(3, rings_at[3])
     second_line(2)
     query_part, key_part = attend_scores_back(chance_t, tq, tk, value_t, at_grad)
@@ -493,6 +502,8 @@
     rows_two[...] = key_part
     split_pairs(rows_one, tq_grad)
     split_pairs(rows_two, tk_grad)
+    store(tq_grad, tq_grad_hbm)
+    store(tk_grad, tk_grad_hbm)
     second_line(1)
     third_line(2)
     second_line(0)
@@ -502,13 +513,24 @@
     third_line(3)
     for number in (2, 1, 0, 3):
         finish(number)
+    store(weight_grads, weight_grads_hbm)
     for copy in sent:
         copy.wait_send()
+    for copy in stored:
+        copy.wait()
 
 
 def hand_over(*refs):
-    for at in range(6):
-        refs[6 + at][...] = refs[at][...]
+    sources, targets, buffers, (in_sem, out_sem) = refs[0:6], refs[6:12], refs[12:18], refs[18:20]
+    arriving = [pltpu.make_async_copy(sources[at], buffers[at], in_sem.at[at]) for at in range(6)]
+    leaving = [pltpu.make_async_copy(buffers[at], targets[at], out_sem.at[at]) for at in range(6)]
+    for copy in arriving:
+        copy.start()
+    for copy, onward in zip(arriving, leaving):
+        copy.wait()
+        onward.start()
+    for onward in leaving:
+        onward.wait()
 
 
 def body(
@@ -528,7 +550,16 @@
     wide, narrow = (TOKENS, WIDTH), (TOKENS, INNER)
     chances = pltpu.VMEM((HEADS, TOKENS, TOKENS), F32)
     dma = pltpu.SemaphoreType.DMA
-    scratch = [pltpu.VMEM(array.shape, BF16) for array in arrays]
+    results = [
+        jax.ShapeDtypeStruct(wide, BF16),
+        jax.ShapeDtypeStruct((INNER, TOKENS), BF16),
+        jax.ShapeDtypeStruct((INNER, TOKENS), BF16),
+        jax.ShapeDtypeStruct((FRAMES, 2, INNER), BF16),
+        jax.ShapeDtypeStruct((FRAMES, 2, INNER), BF16),
+        jax.ShapeDtypeStruct((18, 4, 144), F32),
+    ]
+    buffers = [pltpu.VMEM(result.shape, result.dtype) for result in results]
+    scratch = buffers + [pltpu.VMEM(array.shape, BF16) for array in arrays]
     scratch += [pltpu.VMEM(narrow, BF16)] * 2 + [pltpu.VMEM(wide, BF16)] + [pltpu.VMEM(narrow, BF16)] * 2
     scratch += [pltpu.VMEM(wide, F32)] + [pltpu.VMEM(narrow, F32)] * 2
     scratch += [chances, chances] + [pltpu.VMEM(narrow, BF16)] * 8
@@ -547,20 +578,12 @@
         pltpu.VMEM((4, 7, SHARE_ROWS, 128), BF16),
         pltpu.VMEM((SHARE_ROWS, 128), F32),
     ]
-    scratch += [dma((15,))] + [dma((3, 7))] * 4 + [dma((4,))] * 4 + [dma((4, 6))] * 2 + [dma((4, 3))] * 2 + [dma((4, 7))] * 2
-    results = [
-        jax.ShapeDtypeStruct(wide, BF16),
-        jax.ShapeDtypeStruct((INNER, TOKENS), BF16),
-        jax.ShapeDtypeStruct((INNER, TOKENS), BF16),
-        jax.ShapeDtypeStruct((FRAMES, 2, INNER), BF16),
-        jax.ShapeDtypeStruct((FRAMES, 2, INNER), BF16),
-        jax.ShapeDtypeStruct((18, 4, 144), F32),
-    ]
+    scratch += [dma((15,)), dma((6,))] + [dma((3, 7))] * 4 + [dma((4,))] * 4 + [dma((4, 6))] * 2 + [dma((4, 3))] * 2 + [dma((4, 7))] * 2
     made = pl.pallas_call(
         functools.partial(kernel, grad_scale),
         out_shape=results,
         in_specs=[pl.BlockSpec(memory_space=pl.ANY)] * len(arrays),
-        out_specs=[pl.BlockSpec(memory_space=pltpu.VMEM)] * 6,
+        out_specs=[pl.BlockSpec(memory_space=pl.ANY)] * 6,
         scratch_shapes=scratch,
         compiler_params=pltpu.CompilerParams(
             collective_id=0, has_side_effects=True, vmem_limit_bytes=56 * 2**20
@@ -570,8 +593,9 @@
     input_grad, sq_grad, sk_grad, tq_grad, tk_grad, weight_grads = pl.pallas_call(
         hand_over,
         out_shape=results,
-        in_specs=[pl.BlockSpec(memory_space=pltpu.VMEM)] * 6,
-        out_specs=[pl.BlockSpec(memory_space=pltpu.VMEM)] * 6,
+        in_specs=[pl.BlockSpec(memory_space=pl.ANY)] * 6,
+        out_specs=[pl.BlockSpec(memory_space=pl.ANY)] * 6,
+        scratch_shapes=buffers + [dma((6,)), dma((6,))],
         compiler_params=pltpu.CompilerParams(vmem_limit_bytes=60 * 2**20),
         name="hand_over",
     )(*made)

time: 61.5 us -> 61.5 us (level); the launches traced: 60.3 us -> 61.4 us
  Pallas kernels: 59.7 us -> 60.6 us
    pallas_call x1, Pallas kernels: 57.5 us -> 58.5 us  [body(): pl.pallas_call(functools.partial(kernel, grad_scale), out_shape=results,...]
where the time goes in v8:
time: 61.5 us; the launch traced here: 61.4 us
  Pallas kernels  60.6 us (99%)
  between operations  0.8 us (1%)
    pallas_call x1, Pallas kernels, body(): pl.pallas_call(functools.partial(kernel, grad_scale), out_shape=results,...  58.5 us
    pallas_call x1, Pallas kernels, body(): pl.pallas_call(hand_over, out_shape=results, in_specs=[pl.BlockSpec(memor...  2 us

profile of v8, /device:TPU:4, one launch (start us, length us, event | category | flops | bytes accessed | tf_op | source)
XLA Modules:
  0.0 61.4 jit_solution(17446309865935584772)
XLA Ops:
  0.6 58.5 %block_backward.1 = (bf16[128,1152]{1,0:T(8,128)(2,1)}, bf16[576,128]{1,0:T(8,128)(2,1)}, bf16[576,128]{1,0:T(8,128)(2,1)}, bf16[64,2,576]{2,1,0:T(2,128)(2,1)},...) custom-call(bf16[128,1152]{1,0:T(8,128)(2,1)} %bitcast.22, bf16[576,128]{1,0:T(8,128)(2,1)} %bitcast.26, ...), custom_call_target="tpu_custom_call" | custom-call | tf_op jit(solution)/shard_map/block_backward/pallas_call | solution.py:582
  59.2 2.0 %hand_over.1 = (bf16[128,1152]{1,0:T(8,128)(2,1)}, bf16[576,128]{1,0:T(8,128)(2,1)}, bf16[576,128]{1,0:T(8,128)(2,1)}, bf16[64,2,576]{2,1,0:T(2,128)(2,1)}, bf16...) custom-call(bf16[128,1152]{1,0:T(8,128)(2,1)} %get-tuple-element.18.refs_0_, bf16[576,128]{1,0:T(8,128)(2,1)} %get-tuple-element.19.refs_1_, ...), custom_call_target="tpu_custom_call" | custom-call | tf_op jit(solution)/shard_map/hand_over/pallas_call | solution.py:593

commit v9 on v8

--- a/solution.py
+++ b/solution.py
@@ -17,11 +17,11 @@
 SCORE_SCALE = HEAD_DIM ** (-0.5)
 ROW_BLOCK = 144
 LANES = 256
-PIECE = 4 * ROW_BLOCK + 80
-CUT = 336
-BLOCK_ROWS = ROW_BLOCK + 32
+ROWS_OF = (80, 64)
+REST_ROWS = (48, 32)
+PIECE = (4 * 80 + 48, 4 * 64 + 32)
+CUT = (192, 144)
 SHARE_ROWS = 32
-PAIRS = ((1, 3), (2, 0))
 F32 = jnp.float32
 BF16 = jnp.bfloat16
 MESH = pl.DeviceIdType.MESH
@@ -68,8 +68,8 @@
         for z in range(8):
             for row in range(SHARE_ROWS):
                 at = z * 18 + 9 * group + row - 18
-                place, turn = at // 16, (group - at // 16) % 8
-                source.append(turn * 32 + place // 8 * 16 + at % 16 if 18 <= row < 27 else -1)
+                tile, place = divmod(at // 16, 5)
+                source.append((group - place) % 8 * 32 + tile * 16 + at % 16 if 18 <= row < 27 else -1)
         rest_moves.append(one_hot(source, 256))
     tables = (token_moves, feature_moves, picks, share_moves, np.stack(rest_moves))
     return [jnp.asarray(table, BF16) for table in tables]
@@ -287,96 +287,109 @@
 
     places = (x, y)
     rings = (along_x, along_y)
-    ring_of = {number: ring for ring, numbers in enumerate(PAIRS) for number in numbers}
     slot_half = (0, 1, 1, 0, 0, 1)
 
-    def make_pieces(number, to):
-        rests = None
-        for sub in range(4):
-            side, y_lo_at, x_at = (sub // 2, sub % 2, to) if ring_of[number] == 0 else (to // 2, to % 2, sub)
-            rows = pl.ds(pl.multiple_of((y_lo_at * 4 + x_at) * ROW_BLOCK, 16), ROW_BLOCK)
-            total = dot(factors[number, rows, :], picked[number, side])
-            sums[number, to, sub * ROW_BLOCK : (sub + 1) * ROW_BLOCK, :] = total[:, 0:128].astype(BF16)
-            rest = total[:, 128:256]
-            rests = rest if sub == 0 else rests + pltpu.roll(rest, 16 * sub, 1)
-        beside = jnp.concatenate([pltpu.roll(rests[80:ROW_BLOCK], 64, 1), jnp.zeros((16, 128), F32)], axis=0)
-        sums[number, to, 4 * ROW_BLOCK : PIECE, :] = (rests[0:80] + beside).astype(BF16)
-
-    def piece(number, to, half):
-        return sums.at[number, to, 0:CUT] if half == 0 else sums.at[number, to, CUT:PIECE]
-
-    def slot_ref(number, slot):
-        return arrived.at[number, slot, 0 : (CUT if slot_half[slot] == 0 else PIECE - CUT)]
-
-    def ring_copy(number, slot, source):
-        peer = rings[ring_of[number]](1 if slot % 2 == 0 else 3)
-        return send(source, slot_ref(number, slot), ring_send.at[number, slot], ring_recv.at[number, slot], peer)
+    def make_pieces(number):
+        rests = {}
+        for y_lo_at in range(2):
+            for x_at in range(4):
+                block_rows = (y_lo_at * 4 + x_at) * ROW_BLOCK
+                for side in range(2):
+                    total = dot(factors[number, block_rows : block_rows + ROW_BLOCK, :], picked[number, side])
+                    y_at = 2 * side + y_lo_at
+                    for axis, to, sub in ((0, x_at, y_at), (1, y_at, x_at)):
+                        count = ROWS_OF[axis]
+                        part = total[0:80] if axis == 0 else total[80:ROW_BLOCK]
+                        sums[number, axis, to, sub * count : (sub + 1) * count, :] = part[:, 0:128].astype(BF16)
+                        rest = pltpu.roll(part[:, 128:256], 16 * sub, 1) if sub else part[:, 128:256]
+                        rests[axis, to] = rests[axis, to] + rest if (axis, to) in rests else rest
+        for (axis, to), rest in rests.items():
+            first, count = REST_ROWS[axis], ROWS_OF[axis]
+            beside = pltpu.roll(rest[first:count], 64, 1)
+            if count < 2 * first:
+                beside = jnp.concatenate([beside, jnp.zeros((2 * first - count, 128), F32)], axis=0)
+            sums[number, axis, to, 4 * count : PIECE[axis], :] = (rest[0:first] + beside).astype(BF16)
+
+    def half_rows(axis, half):
+        return slice(0, CUT[axis]) if half == 0 else slice(CUT[axis], PIECE[axis])
+
+    def piece(number, axis, to, half):
+        return sums.at[number, axis, to, half_rows(axis, half)]
+
+    def slot_ref(number, axis, slot):
+        count = CUT[axis] if slot_half[slot] == 0 else PIECE[axis] - CUT[axis]
+        return arrived.at[number, axis, slot, 0:count]
+
+    def ring_copy(number, axis, slot, source):
+        return send(
+            source, slot_ref(number, axis, slot), ring_send.at[number, axis, slot], ring_recv.at[number, axis, slot],
+            rings[axis](1 if slot % 2 == 0 else 3),
+        )
 
     def first_ring(number):
-        place = places[ring_of[number]]
-        after, across, before = (place + 1) % 4, (place + 2) % 4, (place + 3) % 4
         copies = {}
-        make_pieces(number, across)
-        copies[0] = ring_copy(number, 0, piece(number, across, 0))
-        copies[1] = ring_copy(number, 1, piece(number, across, 1))
-        make_pieces(number, after)
-        copies[2] = ring_copy(number, 2, piece(number, after, 1))
-        make_pieces(number, before)
-        copies[3] = ring_copy(number, 3, piece(number, before, 0))
-        make_pieces(number, place)
+        for slot, step, half in ((0, 2, 0), (1, 2, 1), (2, 1, 1), (3, 3, 0)):
+            for axis in range(2):
+                to = (places[axis] + step) % 4
+                copies[axis, slot] = ring_copy(number, axis, slot, piece(number, axis, to, half))
         return copies
 
     def first_relay(number, copies):
-        place = places[ring_of[number]]
-        after, before = (place + 1) % 4, (place + 3) % 4
-        for slot, to, half in ((0, after, 0), (1, before, 1)):
-            copies[slot].wait_recv()
-            ref = piece(number, to, half)
-            ref[...] = (ref[...].astype(F32) + slot_ref(number, slot)[...].astype(F32)).astype(BF16)
-            copies[slot + 4] = ring_copy(number, slot + 4, ref)
+        for slot, step, half in ((0, 1, 0), (1, 3, 1)):
+            for axis in range(2):
+                copies[axis, slot].wait_recv()
+                ref = piece(number, axis, (places[axis] + step) % 4, half)
+                ref[...] = (ref[...].astype(F32) + slot_ref(number, axis, slot)[...].astype(F32)).astype(BF16)
+                copies[axis, slot + 4] = ring_copy(number, axis, slot + 4, ref)
 
     lane_group = lax.broadcasted_iota(jnp.int32, (16, 128), 1) // 16
     share_group = lax.broadcasted_iota(jnp.int32, (8 * SHARE_ROWS, 128), 1) // 16
 
-    def second_place(number):
-        return places[1 - ring_of[number]]
+    def block_two(ref, axis):
+        return ref.at[0 : ROWS_OF[axis] + 16]
 
     def second_line(number):
         copies = rings_at[number]
-        for half, slots in ((0, (3, 4)), (1, (2, 5))):
-            total = piece(number, places[ring_of[number]], half)[...].astype(F32)
-            for slot in slots:
-                copies[slot].wait_recv()
-                total += slot_ref(number, slot)[...].astype(F32)
-            total_one[(0 if half == 0 else CUT) : (CUT if half == 0 else PIECE), :] = total
-        for sub in range(4):
-            sums_two[number, sub, 0:ROW_BLOCK, :] = total_one[sub * ROW_BLOCK : (sub + 1) * ROW_BLOCK, :].astype(BF16)
-            for tile in range(2):
+        seconds[number] = {}
+        for axis in range(2):
+            count = ROWS_OF[axis]
+            for half, slots in ((0, (3, 4)), (1, (2, 5))):
+                total = piece(number, axis, places[axis], half)[...].astype(F32)
+                for slot in slots:
+                    copies[axis, slot].wait_recv()
+                    total += slot_ref(number, axis, slot)[...].astype(F32)
+                total_one[half_rows(axis, half), :] = total
+            for sub in range(4):
+                sums_two[number, axis, sub, 0:count, :] = total_one[sub * count : (sub + 1) * count, :].astype(BF16)
                 packed = jnp.zeros((16, 128), F32)
-                for group in range(8) if tile == 0 else (8,):
-                    start = 4 * ROW_BLOCK + 16 * (group % 5)
-                    turn = (16 * (group % 8) - 16 * sub - (64 if group >= 5 else 0)) % 128
+                for group in range(count // 16):
+                    over = 16 * group >= REST_ROWS[axis]
+                    start = 4 * count + 16 * group - (REST_ROWS[axis] if over else 0)
+                    turn = (16 * group - 16 * sub - (64 if over else 0)) % 128
                     rest = total_one[start : start + 16, :]
                     rest = pltpu.roll(rest, turn, 1) if turn else rest
-                    packed = jnp.where(lane_group == group % 8, rest, packed)
-                start = ROW_BLOCK + 16 * tile
-                sums_two[number, sub, start : start + 16, :] = packed.astype(BF16)
-        seconds[number] = [
-            send(
-                sums_two.at[number, (second_place(number) + step) % 4], arrived_two.at[number, step - 1],
-                ring_two_send.at[number, step - 1], ring_two_recv.at[number, step - 1],
-                rings[1 - ring_of[number]](step),
-            )
-            for step in range(1, 4)
-        ]
+                    packed = jnp.where(lane_group == group, rest, packed)
+                sums_two[number, axis, sub, count : count + 16, :] = packed.astype(BF16)
+            for step in range(1, 4):
+                seconds[number][axis, step] = send(
+                    block_two(sums_two.at[number, axis, (places[1 - axis] + step) % 4], axis),
+                    block_two(arrived_two.at[number, axis, step - 1], axis),
+                    ring_two_send.at[number, axis, step - 1], ring_two_recv.at[number, axis, step - 1],
+                    rings[1 - axis](step),
+                )
 
     def third_line(number):
-        total = sums_two[number, second_place(number)].astype(F32)
-        for step in range(1, 4):
-            seconds[number][step - 1].wait_recv()
-            total += arrived_two[number, step - 1].astype(F32)
-        moved = dot(share_moves[...], total[0:ROW_BLOCK].astype(BF16))
-        ends = total[ROW_BLOCK:BLOCK_ROWS]
+        wholes, ends = [], []
+        for axis in range(2):
+            count = ROWS_OF[axis]
+            total = block_two(sums_two.at[number, axis, places[1 - axis]], axis)[...].astype(F32)
+            for step in range(1, 4):
+                seconds[number][axis, step].wait_recv()
+                total += block_two(arrived_two.at[number, axis, step - 1], axis)[...].astype(F32)
+            wholes.append(total[0:count])
+            ends.append(total[count : count + 16])
+        moved = dot(share_moves[...], jnp.concatenate(wholes, axis=0).astype(BF16))
+        ends = jnp.concatenate(ends, axis=0)
         turned = [ends] + [pltpu.roll(ends, 16 * turn, 1) for turn in range(1, 8)]
         turned = jnp.concatenate(turned, axis=0).astype(BF16)
         for group in range(2):
@@ -406,6 +419,7 @@
 
     def ready(number):
         arrive([feature_copies[number], column_copies[number]])
+        make_pieces(number)
         rings_at[number] = first_ring(number)
 
     def join_pairs(pairs, rows):
@@ -479,24 +493,26 @@
     as_grad[...] = dot_nt(mixed_grad[...], weights[1]).astype(BF16)
     vs_grad[...] = attend_values_back(chance_s, as_grad).astype(BF16)
     column_copies[0] = start_columns(0, vs_grad[...])
+    first_relay(2, rings_at[2])
     arrive(value_z)
     value_t[...] = in_z[1]
     attended_t[...] = attend(chance_t, value_t).astype(BF16)
     column_copies[3] = start_columns(3, attended_t[...])
-    first_relay(2, rings_at[2])
     ready(0)
+    first_relay(1, rings_at[1])
     ready(3)
-    first_relay(1, rings_at[1])
+    first_relay(0, rings_at[0])
+    second_line(2)
     input_grad[...] = (mixed_grad[...].astype(F32) + dot(vs_grad[...], weights[0])).astype(BF16)
     store(input_grad, input_grad_hbm)
-    first_relay(0, rings_at[0])
     query_part, key_part = attend_scores_back(chance_s, sq, sk, value_s, as_grad)
     sq_grad[...] = query_part.astype(BF16).T
     sk_grad[...] = key_part.astype(BF16).T
     store(sq_grad, sq_grad_hbm)
     store(sk_grad, sk_grad_hbm)
     first_relay(3, rings_at[3])
-    second_line(2)
+    second_line(1)
+    third_line(2)
     query_part, key_part = attend_scores_back(chance_t, tq, tk, value_t, at_grad)
     rows_one[...] = query_part
     rows_two[...] = key_part
@@ -504,15 +520,15 @@
     split_pairs(rows_two, tk_grad)
     store(tq_grad, tq_grad_hbm)
     store(tk_grad, tk_grad_hbm)
-    second_line(1)
-    third_line(2)
     second_line(0)
     third_line(1)
     second_line(3)
     third_line(0)
+    finish(2)
+    finish(1)
     third_line(3)
-    for number in (2, 1, 0, 3):
-        finish(number)
+    finish(0)
+    finish(3)
     store(weight_grads, weight_grads_hbm)
     for copy in sent:
         copy.wait_send()
@@ -569,16 +585,16 @@
         pltpu.VMEM((4, WIDTH, 2 * TOKENS), BF16),
         pltpu.VMEM((4, 2, 2 * TOKENS, LANES), BF16),
         pltpu.VMEM((4, 2, TOKENS, LANES), BF16),
-        pltpu.VMEM((4, 4, PIECE, 128), BF16),
-        pltpu.VMEM((4, 6, CUT, 128), BF16),
-        pltpu.VMEM((PIECE, 128), F32),
-        pltpu.VMEM((4, 4, BLOCK_ROWS, 128), BF16),
-        pltpu.VMEM((4, 3, BLOCK_ROWS, 128), BF16),
+        pltpu.VMEM((4, 2, 4, PIECE[0], 128), BF16),
+        pltpu.VMEM((4, 2, 6, CUT[0], 128), BF16),
+        pltpu.VMEM((PIECE[0], 128), F32),
+        pltpu.VMEM((4, 2, 4, 96, 128), BF16),
+        pltpu.VMEM((4, 2, 3, 96, 128), BF16),
         pltpu.VMEM((4, 8, SHARE_ROWS, 128), BF16),
         pltpu.VMEM((4, 7, SHARE_ROWS, 128), BF16),
         pltpu.VMEM((SHARE_ROWS, 128), F32),
     ]
-    scratch += [dma((15,)), dma((6,))] + [dma((3, 7))] * 4 + [dma((4,))] * 4 + [dma((4, 6))] * 2 + [dma((4, 3))] * 2 + [dma((4, 7))] * 2
+    scratch += [dma((15,)), dma((6,))] + [dma((3, 7))] * 4 + [dma((4,))] * 4 + [dma((4, 2, 6))] * 2 + [dma((4, 2, 3))] * 2 + [dma((4, 7))] * 2
     made = pl.pallas_call(
         functools.partial(kernel, grad_scale),
         out_shape=results,

time: 61.5 us -> 60.7 us (0.987)
  Pallas kernels: 60.6 us -> 59.3 us
    pallas_call x1, Pallas kernels: 58.5 us -> 57.3 us  [body(): pl.pallas_call(functools.partial(kernel, grad_scale), out_shape=results,...]
where the time goes in v9:
time: 60.7 us; the launch traced here: 60.1 us
  Pallas kernels  59.3 us (98%)
  between operations  0.8 us (1%)
    pallas_call x1, Pallas kernels, body(): pl.pallas_call(functools.partial(kernel, grad_scale), out_shape=results,...  57.3 us
    pallas_call x1, Pallas kernels, body(): pl.pallas_call(hand_over, out_shape=results, in_specs=[pl.BlockSpec(memor...  2 us

profile of v9, /device:TPU:4, one launch (start us, length us, event | category | flops | bytes accessed | tf_op | source)
XLA Modules:
  0.0 60.1 jit_solution(9756544022459123270)
XLA Ops:
  0.6 57.3 %block_backward.1 = (bf16[128,1152]{1,0:T(8,128)(2,1)}, bf16[576,128]{1,0:T(8,128)(2,1)}, bf16[576,128]{1,0:T(8,128)(2,1)}, bf16[64,2,576]{2,1,0:T(2,128)(2,1)},...) custom-call(bf16[128,1152]{1,0:T(8,128)(2,1)} %bitcast.22, bf16[576,128]{1,0:T(8,128)(2,1)} %bitcast.26, ...), custom_call_target="tpu_custom_call" | custom-call | tf_op jit(solution)/shard_map/block_backward/pallas_call | solution.py:598
  57.9 2.0 %hand_over.1 = (bf16[128,1152]{1,0:T(8,128)(2,1)}, bf16[576,128]{1,0:T(8,128)(2,1)}, bf16[576,128]{1,0:T(8,128)(2,1)}, bf16[64,2,576]{2,1,0:T(2,128)(2,1)}, bf16...) custom-call(bf16[128,1152]{1,0:T(8,128)(2,1)} %get-tuple-element.18.refs_0_, bf16[576,128]{1,0:T(8,128)(2,1)} %get-tuple-element.19.refs_1_, ...), custom_call_target="tpu_custom_call" | custom-call | tf_op jit(solution)/shard_map/hand_over/pallas_call | solution.py:609

commit v10 on v9

--- a/solution.py
+++ b/solution.py
@@ -22,6 +22,8 @@
 PIECE = (4 * 80 + 48, 4 * 64 + 32)
 CUT = (192, 144)
 SHARE_ROWS = 32
+LINE_STEPS = (4, 3, 5, 2, 6, 1, 7)
+PLANE_STEPS = (6, 2, 5, 3, 7, 1, 4)
 F32 = jnp.float32
 BF16 = jnp.bfloat16
 MESH = pl.DeviceIdType.MESH
@@ -236,7 +238,7 @@
 
     def start_z(item, source, target):
         copies = []
-        for step in range(1, 8):
+        for step in LINE_STEPS:
             to = (z + step) % 8
             copies.append(
                 send(
@@ -250,7 +252,7 @@
 
     def start_plane(item, source, target):
         copies = []
-        for step in range(1, 8):
+        for step in PLANE_STEPS:
             to = (q + step) % 8
             copies.append(
                 send(
@@ -370,7 +372,7 @@
                     rest = pltpu.roll(rest, turn, 1) if turn else rest
                     packed = jnp.where(lane_group == group, rest, packed)
                 sums_two[number, axis, sub, count : count + 16, :] = packed.astype(BF16)
-            for step in range(1, 4):
+            for step in (2, 1, 3):
                 seconds[number][axis, step] = send(
                     block_two(sums_two.at[number, axis, (places[1 - axis] + step) % 4], axis),
                     block_two(arrived_two.at[number, axis, step - 1], axis),
@@ -397,18 +399,18 @@
         moved = moved.astype(BF16)
         for z_at in range(8):
             shares[number, z_at] = moved[SHARE_ROWS * z_at : SHARE_ROWS * (z_at + 1)]
-        thirds[number] = [
-            send(
+        thirds[number] = {
+            step: send(
                 shares.at[number, (z + step) % 8], shares_in.at[number, step - 1],
                 share_send.at[number, step - 1], share_recv.at[number, step - 1], along_z(step),
             )
-            for step in range(1, 8)
-        ]
+            for step in LINE_STEPS
+        }
 
     def finish(number):
         total = shares[number, z].astype(F32)
         for step in range(1, 8):
-            thirds[number][step - 1].wait_recv()
+            thirds[number][step].wait_recv()
             total += shares_in[number, step - 1].astype(F32)
         total_share[...] = total * grad_scale
         weight_grads[:, number, 0:128] = total_share[0:18, :]

time: 60.7 us -> 58.9 us (0.970)
  Pallas kernels: 59.3 us -> 57.4 us
    pallas_call x1, Pallas kernels: 57.3 us -> 55.4 us  [body(): pl.pallas_call(functools.partial(kernel, grad_scale), out_shape=results,...]
where the time goes in v10:
time: 58.9 us; the launch traced here: 58.2 us
  Pallas kernels  57.4 us (97%)
  between operations  0.8 us (1%)
    pallas_call x1, Pallas kernels, body(): pl.pallas_call(functools.partial(kernel, grad_scale), out_shape=results,...  55.4 us
    pallas_call x1, Pallas kernels, body(): pl.pallas_call(hand_over, out_shape=results, in_specs=[pl.BlockSpec(memor...  2 us

profile of v10, /device:TPU:4, one launch (start us, length us, event | category | flops | bytes accessed | tf_op | source)
XLA Modules:
  0.0 58.2 jit_solution(349314334225874388)
XLA Ops:
  0.6 55.4 %block_backward.1 = (bf16[128,1152]{1,0:T(8,128)(2,1)}, bf16[576,128]{1,0:T(8,128)(2,1)}, bf16[576,128]{1,0:T(8,128)(2,1)}, bf16[64,2,576]{2,1,0:T(2,128)(2,1)},...) custom-call(bf16[128,1152]{1,0:T(8,128)(2,1)} %bitcast.22, bf16[576,128]{1,0:T(8,128)(2,1)} %bitcast.26, ...), custom_call_target="tpu_custom_call" | custom-call | tf_op jit(solution)/shard_map/block_backward/pallas_call | solution.py:600
  56.0 2.0 %hand_over.1 = (bf16[128,1152]{1,0:T(8,128)(2,1)}, bf16[576,128]{1,0:T(8,128)(2,1)}, bf16[576,128]{1,0:T(8,128)(2,1)}, bf16[64,2,576]{2,1,0:T(2,128)(2,1)}, bf16...) custom-call(bf16[128,1152]{1,0:T(8,128)(2,1)} %get-tuple-element.18.refs_0_, bf16[576,128]{1,0:T(8,128)(2,1)} %get-tuple-element.19.refs_1_, ...), custom_call_target="tpu_custom_call" | custom-call | tf_op jit(solution)/shard_map/hand_over/pallas_call | solution.py:611

commit v11 on v10

--- a/solution.py
+++ b/solution.py
@@ -212,7 +212,7 @@
         loads.append(copy)
 
     barrier = pltpu.get_barrier_semaphore()
-    greeted = [along_z(step) for step in range(1, 8)] + [in_the_plane(step) for step in range(1, 8)]
+    greeted = [along_z(step) for step in LINE_STEPS] + [in_the_plane(step) for step in PLANE_STEPS]
     greeted += [device(y_hi_at=1 - y_hi, y_lo_at=1 - y_lo), sibling]
     for peer in greeted:
         pl.semaphore_signal(barrier, inc=1, device_id=peer, device_id_type=MESH)

time: 58.9 us -> 58.9 us (level)
  no operation moved by 1% of the time
where the time goes in v11:
time: 58.9 us; the launch traced here: 58.1 us
  Pallas kernels  57.3 us (97%)
  between operations  0.8 us (1%)
    pallas_call x1, Pallas kernels, body(): pl.pallas_call(functools.partial(kernel, grad_scale), out_shape=results,...  55.3 us
    pallas_call x1, Pallas kernels, body(): pl.pallas_call(hand_over, out_shape=results, in_specs=[pl.BlockSpec(memor...  2 us

profile of v11, /device:TPU:4, one launch (start us, length us, event | category | flops | bytes accessed | tf_op | source)
XLA Modules:
  0.0 58.1 jit_solution(17524428026029280618)
XLA Ops:
  0.6 55.3 %block_backward.1 = (bf16[128,1152]{1,0:T(8,128)(2,1)}, bf16[576,128]{1,0:T(8,128)(2,1)}, bf16[576,128]{1,0:T(8,128)(2,1)}, bf16[64,2,576]{2,1,0:T(2,128)(2,1)},...) custom-call(bf16[128,1152]{1,0:T(8,128)(2,1)} %bitcast.22, bf16[576,128]{1,0:T(8,128)(2,1)} %bitcast.26, ...), custom_call_target="tpu_custom_call" | custom-call | tf_op jit(solution)/shard_map/block_backward/pallas_call | solution.py:600
  56.0 2.0 %hand_over.1 = (bf16[128,1152]{1,0:T(8,128)(2,1)}, bf16[576,128]{1,0:T(8,128)(2,1)}, bf16[576,128]{1,0:T(8,128)(2,1)}, bf16[64,2,576]{2,1,0:T(2,128)(2,1)}, bf16...) custom-call(bf16[128,1152]{1,0:T(8,128)(2,1)} %get-tuple-element.18.refs_0_, bf16[576,128]{1,0:T(8,128)(2,1)} %get-tuple-element.19.refs_1_, ...), custom_call_target="tpu_custom_call" | custom-call | tf_op jit(solution)/shard_map/hand_over/pallas_call | solution.py:611
